TPU v7x, 128 devices: a whole 4x4x4 slice. The times are simulated.
128 devices in a mesh: gz: 8 (over x, core), gy: 4 (over y), gx: 4 (over z).
Axes of the slice: x: 4, y: 4, z: 4, core: 2. Of those that a mesh axis runs over, the one named last changes fastest.
Arguments:
- charges: float32 [512, 512, 512], P('gz', 'gy', 'gx'), may hold values from -6 to 6
- level_taps: float32 [3, 9], replicated, may hold values from -1 to 1
- top_taps: float32 [64], replicated, may hold values from -0.5 to 0.5
Outputs:
- potential: float32 [512, 512, 512], P('gz', 'gy', 'gx')
All inputs are finite; a program needn't handle non-finite values.
Results may differ from a plain program's by a relative error of at most 0.00011.
Values sent between devices are 32-bit elements; how exact they have to be, the bound alone decides.
No kernel may reach another device: no remote copies, remote signals or barrier semaphores. Data moves between devices by JAX's collectives and lax.ppermute only.
A program may use at most 128 MiB of HBM per device.

v0:
```python
import jax
import jax.numpy as jnp
import numpy as np
from jax import lax
from jax.experimental import pallas as pl
from jax.experimental.pallas import tpu as pltpu
from jax.sharding import PartitionSpec as P

AXES = ("gz", "gy", "gx")
F32 = jnp.float32
BF16 = jnp.bfloat16
NN = (((1,), (0,)), ((), ()))
NT = (((1,), (1,)), ((), ()))
ANY = pl.BlockSpec(memory_space=pl.ANY)
SMEM = pl.BlockSpec(memory_space=pltpu.SMEM)
VMEM = pl.BlockSpec(memory_space=pltpu.VMEM)


def phi(dist):
    dist = np.abs(dist)
    return np.where(
        dist == 0, 1.0, np.where(dist == 1, 0.5625, np.where(dist == 3, -0.0625, 0.0))
    )


def restrict_whole(size):
    rows = np.arange(size // 2)[:, None]
    cols = np.arange(size)[None, :]
    return phi(cols - 2 * rows)


def rows_of(whole, first, count):
    picked = np.zeros((count, whole.shape[1]))
    for r in range(count):
        if 0 <= first + r < whole.shape[0]:
            picked[r] = whole[first + r]
    return picked


def chain_tables(size, count):
    own0 = size // count
    first = restrict_whole(size)
    second = restrict_whole(size // 2) @ first
    stack = []
    for place in range(count):
        parts = []
        for whole, own, low, high in ((first, own0 // 2, 1, 2), (second, own0 // 4, 2, 3)):
            cols = whole[:, place * own0 : (place + 1) * own0]
            at = place * own
            parts.append(rows_of(cols, at, own))
            to_low = [np.zeros((4 - low, own0)), rows_of(cols, at - low, low)]
            to_high = [rows_of(cols, at + own, high), np.zeros((4 - high, own0))]
            parts.extend(to_low * 2 + to_high * 2)
        stack.append(np.concatenate(parts))
    return np.stack(stack).astype(jnp.bfloat16)


def chain_rows(size, count):
    own0 = size // count
    first = restrict_whole(size)
    second = restrict_whole(size // 2) @ first
    stacks = []
    for whole, own, low, high, rows in ((first, own0 // 2, 1, 2, 80), (second, own0 // 4, 2, 3, 48)):
        stack = np.zeros((count, rows, own0))
        for place in range(count):
            cols = whole[:, place * own0 : (place + 1) * own0]
            stack[place, : own + low + high] = rows_of(cols, place * own - low, own + low + high)
        stacks.append(stack.astype(jnp.bfloat16))
    return stacks


def prolong_table(total, count, low, high, from_low, from_high, shape):
    own = total // count
    stack = []
    for place in range(count):
        i = np.arange(-low, own + high)[:, None]
        coarse = np.arange(-from_low, own // 2 + from_high)[None, :]
        where = i + place * own
        table = phi(i - 2 * coarse) * ((where >= 0) & (where < total))
        whole = np.zeros(shape)
        whole[: table.shape[0], : table.shape[1]] = table
        stack.append(whole)
    return np.stack(stack)


def shift(value, name, step):
    count = lax.axis_size(name)
    return lax.ppermute(value, name, [(i, (i + step) % count) for i in range(count)])


def split(x):
    high = x.astype(BF16)
    return high, (x - high.astype(F32)).astype(BF16)


def dot(a, b, dims=NN):
    return lax.dot_general(a, b, dims, preferred_element_type=F32)


def mm(a, b):
    a_high, a_low = split(a)
    b_high, b_low = split(b)
    return dot(a_high, b_high) + (dot(a_low, b_high) + dot(a_high, b_low))


def exact_left(table, x):
    high, low = split(x)
    return dot(table, high) + dot(table, low)


def exact_right(x, table):
    high, low = split(x)
    return dot(high, table) + dot(low, table)


def neighbours(name):
    place = lax.axis_index(name)
    count = lax.axis_size(name)
    return (place > 0).astype(F32), (place < count - 1).astype(F32)


def call(body, outs, us, in_specs, out_specs, after=(), carry=(), vmem=8, **kwargs):
    count, kept = len(in_specs), len(outs)
    total = count + len(after) + len(carry)
    shapes = [jax.ShapeDtypeStruct(s, F32) for s in outs]
    shapes += [jax.ShapeDtypeStruct(a.shape, a.dtype) for a in carry]

    def run(*refs):
        inner = refs[total:]
        body(*refs[:count], *inner[:kept], *inner[kept + len(carry) :])

    kernel = pl.pallas_call(
        run,
        out_shape=shapes,
        in_specs=[*in_specs, *[ANY] * (total - count)],
        out_specs=[*out_specs, *[ANY] * len(carry)],
        input_output_aliases={count + len(after) + k: kept + k for k in range(len(carry))},
        compiler_params=pltpu.CompilerParams(vmem_limit_bytes=vmem * 1024 * 1024),
        cost_estimate=pl.CostEstimate(
            flops=int(us * 1.15e10), bytes_accessed=int(us * 3.6e8), transcendentals=0
        ),
        **kwargs,
    )
    return lambda *args: kernel(*args, *after, *carry)


def grid_of(rows, cols):
    shape = (rows, cols)
    return lax.broadcasted_iota(jnp.int32, shape, 0), lax.broadcasted_iota(jnp.int32, shape, 1)


def lane_of(rows):
    return grid_of(rows, 128)[1]


def pack(first, second):
    return jnp.where(grid_of(8, 128)[0] < 4, first, second)


def unpack_low(tile, part):
    tile = tile if part else pltpu.roll(tile, 4, 0)
    return jnp.where(grid_of(8, 128)[0] >= 4, tile, 0.0)


def unpack_high(tile, part):
    tile = pltpu.roll(tile, 4, 0) if part else tile
    return jnp.where(grid_of(8, 128)[0] < 4, tile, 0.0)


def along_z(taps, count, first, last, load):
    planes = {}

    def get(i):
        if not 0 <= i < count:
            return None
        if i not in planes:
            planes[i] = load(i)
        return planes[i]

    for k in range(first, last + 1):
        total = None
        for d in range(9):
            below, above = get(k - d), (get(k + d) if d else None)
            pair = below if above is None else above if below is None else below + above
            if pair is None:
                continue
            pair = pair * taps[d]
            total = pair if total is None else total + pair
        yield k, total


def coarse_z_body(g, own1, own2, low, high):
    has_low, has_high = neighbours("gz")

    @pl.loop(0, 16)
    def _(chunk):
        rows = pl.ds(pl.multiple_of(8 * chunk, 8), 8)

        def weigh(at, count, get, low_at=0):
            total = None
            for offsets, weight in (((0,), 1.0), ((-1, 1), 0.5625), ((-3, 3), -0.0625)):
                part = None
                for o in offsets:
                    if low_at <= 2 * at + o < count:
                        value = get(2 * at + o)
                        part = value if part is None else part + value
                if part is not None:
                    part = part if weight == 1.0 else part * weight
                    total = part if total is None else total + part
            return total

        planes = {}

        def get(i):
            if i not in planes:
                planes[i] = g[i, rows, :]
            return planes[i]

        first = {}
        for j in range(-1, 34):
            first[j] = weigh(j, 64, get)
            if 0 <= j < 32:
                own1[j, rows, :] = first[j]
        for j, has in ((-1, has_low), (32, has_high), (33, has_high)):
            first[j] = first[j] * has
        low[0, rows, :] = first[-1]
        high[0, rows, :] = first[32]
        high[1, rows, :] = first[33]
        for k in range(-2, 19):
            value = weigh(k, 34, lambda j: first[j], -1)
            if k < 0:
                low[3 + k, rows, :] = value * has_low
            elif k < 16:
                own2[k, rows, :] = value
            else:
                high[k - 14, rows, :] = value * has_high


def coarse_z(g):
    return call(
        coarse_z_body,
        [(32, 128, 128), (16, 128, 128), (3, 128, 128), (5, 128, 128)],
        us=1.5,
        vmem=16,
        in_specs=[VMEM],
        out_specs=[VMEM] * 4,
    )(g)


def coarse_x_body(table, own1, own2, from_high, from_low, out1, out2, low, high):
    own_table = table[lax.axis_index("gx")]
    doubled = jnp.concatenate([own_table, own_table], axis=1)

    def work(source, out, at, pair, first, rows, extra=(None, None)):
        values = [source[2 * pair + k] for k in range(2)]
        values = [v if e is None else v + e for v, e in zip(values, extra)]
        wide = jnp.concatenate(split(jnp.concatenate(values, axis=0)), axis=1)
        full = dot(doubled[first : first + rows + 16], wide, NT)
        left, right = full[:, 0:128], full[:, 128:256]
        out[2 * pair] = left[:rows]
        out[2 * pair + 1] = right[:rows]
        low[at + pair] = pack(left[rows : rows + 8], right[rows : rows + 8])
        high[at + pair] = pack(left[rows + 8 :], right[rows + 8 :])

    for pair in range(16):
        extra = [from_low[0], from_low[1]] if pair == 0 else [None, None]
        if pair == 15:
            extra = [None, from_high[0]]
        work(own1, out1, 0, pair, 0, 64, extra)
    for pair in range(8):
        extra = [from_low[2], from_low[3]] if pair == 0 else [None, None]
        if pair == 1:
            extra = [from_low[4], None]
        if pair == 7:
            extra = [from_high[1], from_high[2]]
        work(own2, out2, 16, pair, 80, 32, extra)


def coarse_x(table, own1, own2, from_high, from_low, carry):
    return call(
        coarse_x_body,
        [(32, 64, 128), (16, 32, 128), (24, 8, 128), (24, 8, 128)],
        us=2,
        vmem=16,
        in_specs=[VMEM] * 5,
        out_specs=[VMEM] * 4,
        carry=carry,
    )(table, own1, own2, from_high, from_low)


def stacked(own, from_low, from_high, first, planes):
    parts = []
    for k in range(planes):
        z = first + k
        at, part = divmod(z, 2)
        rows = own.shape[1]
        parts.append(own[z, 0:8] + unpack_high(from_low[at], part))
        parts.append(own[z, 8 : rows - 8])
        parts.append(own[z, rows - 8 : rows] + unpack_low(from_high[at], part))
    return jnp.concatenate(parts, axis=0)


def mm_turned(table, value):
    t_high, t_low = split(table)
    high, low = split(value)
    wide = jnp.concatenate([t_high, t_low, t_high], axis=1)
    return dot(wide, jnp.concatenate([high, high, low], axis=1), NT)


def top_y_body(table, table1, own1, own2, from_high, from_low, top, near, near1, up, down, far):
    half = from_low.at[16:24], from_high.at[16:24]
    full = mm_turned(table[...], stacked(own2, *half, 0, 16))
    top[...] = full[0:24]
    up[0:24] = full[24:48]
    far[...] = full[48:72]
    down[0:24] = full[72:96]
    near[...] = full[96:136]
    down[24:40] = full[136:152]
    up[24:40] = full[152:168]
    for q in range(8):
        full = mm_turned(table1[...], stacked(own1, from_low, from_high, 4 * q, 4))
        near1[:, 256 * q : 256 * q + 256] = full[0:72]
        lanes = slice(256 * (q % 2), 256 * (q % 2) + 256)
        rows = slice(40 + 16 * (q // 2), 56 + 16 * (q // 2))
        down[rows, lanes] = full[72:88]
        up[rows, lanes] = full[88:104]


def top_y(table, table1, own1, own2, from_high, from_low, carry):
    return call(
        top_y_body,
        [(24, 512), (40, 512), (72, 2048), (104, 512), (104, 512), (24, 512)],
        us=1.5,
        in_specs=[VMEM] * 6,
        out_specs=[VMEM] * 6,
        carry=carry,
    )(table, table1, own1, own2, from_high, from_low)


def top_x_body(
    ttable, ntable, table1, edges, top, near, near1, f_low, f_high, f_far,
    otop, onear, onear1, up, down, far,
):
    total = top[...] + f_low[0:24] + (f_high[0:24] + f_far[...])
    extended = jnp.concatenate(
        [near[0:16] + f_low[24:40], near[16:24], near[24:40] + f_high[24:40]], axis=0
    )
    stacked = jnp.concatenate([total[:, 128 * t : 128 * t + 128] for t in range(4)], axis=0)
    full = mm(stacked, ttable[...])
    otop[...] = full[:, 0:128]
    up[0:96] = full[:, 128:256]
    far[...] = full[:, 256:384]
    down[0:96] = full[:, 384:512]
    stacked = jnp.concatenate([extended[:, 128 * t : 128 * t + 128] for t in range(4)], axis=0)
    full = mm(stacked, ntable[...])
    onear[...] = full[:, 0:256]
    down[96:256] = full[:, 256:384]
    up[96:256] = full[:, 384:512]
    tiles = []
    for t in range(16):
        lanes = slice(128 * t, 128 * t + 128)
        rows = slice(40 + 16 * (t // 4), 56 + 16 * (t // 4))
        part = slice(128 * (t % 4), 128 * (t % 4) + 128)
        parts = [near1[0:16, lanes] + f_low[rows, part], near1[16:56, lanes]]
        parts.append(near1[56:72, lanes] + f_high[rows, part])
        tiles.append(jnp.concatenate(parts, axis=0))
    for q in range(4):
        full = mm(jnp.concatenate(tiles[4 * q : 4 * q + 4], axis=1), edges[...])
        down[256 + 72 * q : 328 + 72 * q] = full[:, 0:128]
        up[256 + 72 * q : 328 + 72 * q] = full[:, 128:256]
    for t in range(16):
        full = mm(tiles[t], table1[...])
        onear1[2 * t] = full[:, 0:128]
        onear1[2 * t + 1] = full[:, 128:256]


def top_x(ttable, ntable, table1, edges, top, near, near1, f_low, f_high, f_far, after):
    return call(
        top_x_body,
        [(96, 128), (160, 256), (32, 72, 128), (544, 128), (544, 128), (96, 128)],
        us=2,
        in_specs=[VMEM] * 10,
        out_specs=[VMEM] * 6,
        after=after,
    )(ttable, ntable, table1, edges, top, near, near1, f_low, f_high, f_far)


def folded(values):
    lane = lane_of(values[0].shape[0])
    tail = jnp.zeros_like(values[0])
    for k, value in enumerate(values):
        tail = jnp.where(lane // 4 == k, pltpu.roll(value, (64 + 4 * k) % 128, 1), tail)
    packed = []
    for k in range(0, len(values), 2):
        second = pltpu.roll(values[k + 1], 64, 1) if k + 1 < len(values) else jnp.zeros_like(tail)
        packed.append(jnp.where(lane < 64, values[k], second))
    return [*packed, tail]


def unfold(buffer, k, tail):
    first = buffer[72 * (k // 2) : 72 * (k // 2) + 72]
    lane = lane_of(72)
    first = pltpu.roll(first, 64, 1) if k % 2 else first
    last = pltpu.roll(buffer[72 * tail : 72 * tail + 72], (64 - 4 * k) % 128, 1)
    return jnp.where(lane < 64, first, jnp.where(lane < 68, last, 0.0))


def one_z(taps, ext, from_high, from_low, out, up, down):
    has_low, has_high = neighbours("gz")
    weights = [taps[1, d] * 0.5 for d in range(9)]
    group = lane_of(8) // 16

    @pl.loop(0, 9)
    def _(chunk):
        rows = pl.ds(pl.multiple_of(8 * chunk, 8), 8)

        def load(z):
            q, g = z // 8, z % 8
            at = pl.ds(pl.multiple_of(256 + 72 * q + 8 * chunk, 8), 8)
            a = jnp.where(group == g, from_low[at, :], 0.0)
            b = jnp.where(group == g, from_high[at, :], 0.0)
            if g:
                a = pltpu.roll(a, 128 - 16 * g, 1)
            b = pltpu.roll(b, (57 - 16 * g) % 128, 1)
            return ext[z, rows, :] + (a + b)

        lows, highs = [], []
        for k, total in along_z(weights, 32, -8, 39, load):
            if k < 2:
                lows.append(total * has_low)
            if k > 30:
                highs.append(total * has_high)
            if -1 <= k < 34:
                out[k + 1, rows, :] = total * (has_low if k < 0 else has_high if k > 31 else 1.0)
        for values, buffer in ((lows, down), (highs, up)):
            for k, value in enumerate(folded(values)):
                buffer[pl.ds(pl.multiple_of(72 * k + 8 * chunk, 8), 8), :] = value


def top_z_body(
    taps, tcoef, ncoef, top, near, ext, f_low, f_high, f_far, parts, partner, onear, out1, up, down
):
    total = top[...] + f_low[0:96] + (f_high[0:96] + f_far[...])
    group = lane_of(24) // 32
    planes = []
    for z in range(16):
        tile = total[24 * (z // 4) : 24 * (z // 4) + 24]
        part = jnp.where(group == z % 4, tile, 0.0)
        part = part + pltpu.roll(part, 32, 1)
        planes.append(part + pltpu.roll(part, 64, 1))
    for step in range(8):
        out = partner if step // 4 else parts
        for quarter in range(4):
            value = None
            for z in range(16):
                at = (step * 4 + quarter) * 16 + z
                part = planes[z] * tcoef[at : at + 1, :]
                value = part if value is None else value + part
            rows = 96 * (step % 4) + 24 * quarter
            out[rows : rows + 24] = value
    lane = lane_of(40)
    planes = []
    for z in range(16):
        tile, q = z // 4, z % 4
        rows = slice(40 * tile, 40 * tile + 40)
        part = near[rows, 128 * (q // 2) : 128 * (q // 2) + 128]
        part = jnp.where(lane // 64 == q % 2, part, 0.0)
        low = jnp.where(lane // 32 == q, f_low[96 + 40 * tile : 136 + 40 * tile], 0.0)
        high = jnp.where(lane // 32 == q, f_high[96 + 40 * tile : 136 + 40 * tile], 0.0)
        if q % 2:
            part = pltpu.roll(part, 64, 1)
        if q:
            low = pltpu.roll(low, 128 - 32 * q, 1)
        high = pltpu.roll(high, (26 - 32 * q) % 128, 1)
        part = part + (low + high)
        planes.append(part + pltpu.roll(part, 64, 1))
    for out, base, count, first, offset in (
        (onear, 0, 11, -2, 0),
        (down, 11, 6, -8, 432),
        (up, 17, 5, 14, 432),
    ):
        for p in range(count):
            value = None
            for z in range(16):
                r = first + 2 * p
                if min(abs(r - z), abs(r + 1 - z)) > 8:
                    continue
                at = (base + p) * 16 + z
                part = planes[z] * ncoef[at : at + 1, :]
                value = part if value is None else value + part
            out[offset + 40 * p : offset + 40 * p + 40] = value

    one_z(taps, ext, f_high, f_low, out1, up, down)


def top_z(taps, tcoef, ncoef, top, near, ext, f_low, f_high, f_far, after):
    return call(
        top_z_body,
        [(384, 128), (384, 128), (440, 128), (35, 72, 128), (632, 128), (672, 128)],
        us=4,
        in_specs=[SMEM] + [VMEM] * 8,
        out_specs=[VMEM] * 6,
        after=after,
    )(taps, tcoef, ncoef, top, near, ext, f_low, f_high, f_far)


def top_sum_body(own, other, *outs):
    for k, out in enumerate(outs):
        rows = slice(96 * k, 96 * k + 96)
        out[...] = own[rows] + other[rows]


def top_sum(own, other, after):
    return call(
        top_sum_body,
        [(96, 128)] * 4,
        us=0.3,
        in_specs=[VMEM] * 2,
        out_specs=[VMEM] * 4,
        after=after,
    )(own, other)


def rise_body(
    py2, px2, mask2, py1, px1, mask1, py0, px0, top, p1, p2, p3, near2, f_low, f_high,
    near1, out, middle,
):
    z, y, x = [lax.axis_index(name) for name in AXES]
    py2, py1, py0 = py2[y], py1[y], py0[y]
    px2, px1, px0 = px2[x], px1[x], px0[x]
    total = (top[...] + p1[...]) + (p2[...] + p3[...])
    lane = lane_of(40)
    wide = jnp.concatenate([total[24 * q : 24 * q + 24] for q in range(4)], axis=1)
    tile = exact_left(py2, wide)
    rows = jnp.concatenate([tile[:, 128 * q : 128 * q + 128] for q in range(4)], axis=0)
    rows = exact_right(rows, px2)
    two = []
    for k in range(13):
        q, g = divmod(k, 4)
        part = rows[40 * q : 40 * q + 40, 128 * (g // 2) : 128 * (g // 2) + 128]
        part = jnp.where(lane // 64 == g % 2, part, 0.0)
        two.append(part + pltpu.roll(part, 64, 1))
    values = []
    for p in range(11):
        even = two[p + 1]
        if p < 10:
            odd = 0.5625 * (two[p + 1] + two[p + 2]) - 0.0625 * (two[p] + two[p + 3])
        else:
            odd = jnp.zeros_like(even)
        value = jnp.where(lane < 64, even, odd) * mask2[z, p : p + 1, :]
        value = value + near2[40 * p : 40 * p + 40]
        if p < 5:
            value = value + f_low[432 + 40 * p : 472 + 40 * p]
        else:
            value = value + f_high[432 + 40 * (p - 5) : 472 + 40 * (p - 5)]
        values.append(value)
    tile = exact_left(py1, jnp.concatenate(values, axis=1))
    rows = jnp.concatenate([tile[:, 128 * p : 128 * p + 128] for p in range(11)], axis=0)
    rows = exact_right(rows, px1)
    one = []
    for p in range(11):
        one.append(rows[72 * p : 72 * p + 72, 0:128])
        one.append(rows[72 * p : 72 * p + 72, 128:256])
    for f in range(35):
        if f % 2:
            value = one[(f + 3) // 2]
        else:
            h = f // 2
            value = 0.5625 * (one[h + 1] + one[h + 2]) - 0.0625 * (one[h] + one[h + 3])
        value = value * mask1[z, f] + near1[f]
        if f < 9:
            value = value + unfold(f_low, f, 5)
        elif f > 24:
            value = value + unfold(f_high, f - 25, 5)
        middle[72 * f : 72 * f + 72] = value
    doubled = jnp.concatenate([px0, px0], axis=0)
    left = jnp.concatenate([py0, py0], axis=1)
    for group in range(5):
        part = middle[504 * group : 504 * group + 504]
        part = dot(jnp.concatenate(split(part), axis=1), doubled)
        wide = jnp.concatenate([part[72 * k : 72 * k + 72] for k in range(7)], axis=1)
        full = dot(left, jnp.concatenate(split(wide), axis=0))
        for k in range(7):
            out[7 * group + k] = full[:, 128 * k : 128 * k + 128]


def rise(tables, top, others, near2, f_low, f_high, near1):
    return call(
        rise_body,
        [(35, 128, 128)],
        us=5,
        in_specs=[VMEM] * 5 + [SMEM] + [VMEM] * 10,
        out_specs=[VMEM],
        scratch_shapes=[pltpu.VMEM((2520, 128), F32)],
    )(*tables, top, *others, near2, f_low, f_high, near1)[0]


def near_z_body(taps, g, own, low, high):
    has_low, has_high = neighbours("gz")
    weights = [taps[0, d] for d in range(9)]

    @pl.loop(0, 16)
    def _(chunk):
        rows = pl.ds(pl.multiple_of(8 * chunk, 8), 8)
        for k, total in along_z(weights, 64, -8, 71, lambda i: g[i, rows, :]):
            if k < 0:
                low[k + 8, rows, :] = total * has_low
            elif k < 64:
                own[k, rows, :] = total
            else:
                high[k - 64, rows, :] = total * has_high


def near_z(taps, g, after):
    return call(
        near_z_body,
        [(64, 128, 128), (8, 128, 128), (8, 128, 128)],
        us=6,
        vmem=16,
        in_specs=[SMEM, VMEM],
        out_specs=[VMEM] * 3,
        after=after,
    )(taps, g)


def taps_at(taps, level, dist):
    value = jnp.zeros(dist.shape, F32)
    for d in range(9):
        value = jnp.where(dist == d, taps[level, d], value)
    return value


def near_at(taps, dist):
    return taps_at(taps, 0, jnp.abs(dist))


def near_x_body(taps, g, from_high, from_low, own, low, high):
    has_low, has_high = neighbours("gx")
    row, col = grid_of(128, 128)
    edge = near_at(taps, row - col + 8) * jnp.where(col < 8, has_low, 0.0)
    edge = edge + near_at(taps, row - col - 120) * jnp.where((col >= 8) & (col < 16), has_high, 0.0)
    upper, lower = split(jnp.concatenate([near_at(taps, row - col), edge], axis=1))
    table = jnp.concatenate([upper, upper], axis=0)

    def work(k, q, j, extra=None):
        value = g[k] if extra is None else g[k] + extra
        first, second = split(value)
        full = dot(jnp.concatenate([first, second], axis=1), table) + dot(first, lower)
        own[k] = full[:, 0:128]
        low[q, :, 8 * j : 8 * j + 8] = full[:, 128:136]
        high[q, :, 8 * j : 8 * j + 8] = full[:, 136:144]

    for j in range(16):
        work(j, 0, j, from_low[j] if j < 8 else None)

    @pl.loop(1, 3)
    def _(q):
        for j in range(16):
            work(16 * q + j, q, j)

    for j in range(16):
        work(48 + j, 3, j, from_high[j - 8] if j >= 8 else None)


def near_x(taps, g, from_high, from_low, after):
    return call(
        near_x_body,
        [(64, 128, 128), (4, 128, 128), (4, 128, 128)],
        us=5,
        vmem=16,
        in_specs=[SMEM] + [VMEM] * 3,
        out_specs=[VMEM] * 3,
        after=after,
    )(taps, g, from_high, from_low)


def near_y_body(taps, g, from_high, from_low, own, low, high):
    has_low, has_high = neighbours("gy")
    row, col = grid_of(8, 128)
    value = jnp.concatenate(
        [
            near_at(taps, grid_of(128, 128)[0] - grid_of(128, 128)[1]),
            near_at(taps, row - col - 8) * has_low,
            near_at(taps, row - col + 128) * has_high,
        ],
        axis=0,
    )
    upper, lower = split(value)
    wide_table = jnp.concatenate([upper, upper], axis=1)
    lane = lane_of(128)

    def load(q, j):
        left = pltpu.roll(from_low[q], (128 - 8 * j) % 128, 1)
        right = pltpu.roll(from_high[q], (120 - 8 * j) % 128, 1)
        sides = jnp.where(lane < 8, left, jnp.where(lane >= 120, right, 0.0))
        return g[16 * q + j] + sides

    @pl.loop(0, 4)
    def _(q):
        for pair in range(8):
            values = [load(q, 2 * pair + k) for k in range(2)]
            first, second = split(jnp.concatenate(values, axis=1))
            full = dot(wide_table, jnp.concatenate([first, second], axis=0))
            full = full + dot(lower, first)
            for k in range(2):
                at = 16 * q + 2 * pair + k
                part = full[:, 128 * k : 128 * k + 128]
                own[at] = part[0:128]
                low[at] = part[128:136]
                high[at] = part[136:144]


def near_y(taps, g, from_high, from_low, after):
    return call(
        near_y_body,
        [(64, 128, 128), (64, 8, 128), (64, 8, 128)],
        us=4,
        vmem=16,
        in_specs=[SMEM] + [VMEM] * 3,
        out_specs=[VMEM] * 3,
        after=after,
    )(taps, g, from_high, from_low)


def finest_body(near, from_high, from_low, coarse, out):
    step = pl.program_id(0)
    at = 8 * step
    planes = [coarse[at + h] for h in range(11)]
    for k in range(16):
        h = k // 2
        value = planes[h + 1]
        if k % 2:
            value = 0.5625 * (value + planes[h + 2]) - 0.0625 * (planes[h] + planes[h + 3])
        value = value + near[16 * step + k]
        out[k, 0:8] = value[0:8] + from_low[16 * step + k]
        out[k, 8:120] = value[8:120]
        out[k, 120:128] = value[120:128] + from_high[16 * step + k]


def finest(near, from_high, from_low, coarse):
    return call(
        finest_body,
        [(64, 128, 128)],
        us=4,
        vmem=16,
        grid=(4,),
        in_specs=[VMEM] * 4,
        out_specs=[pl.BlockSpec((16, 128, 128), lambda i: (i, 0, 0))],
    )(near, from_high, from_low, coarse)[0]


def phi_at(dist):
    dist = jnp.abs(dist)
    return jnp.where(
        dist == 0, 1.0, jnp.where(dist == 1, 0.5625, jnp.where(dist == 3, -0.0625, 0.0))
    ).astype(F32)


def toeplitz(line, rows, offset):
    line = pltpu.roll(line, lax.rem(192 - offset, 128), 1)
    wide = jnp.broadcast_to(line[0:1], (rows, 128))
    return pltpu.roll(wide, 0, 1, stride=1, stride_axis=0)


def tables_body(taps, top_taps, rows1, rows2, ytab, ttab, ntab, tcoef, ncoef, oney, onex, edges):
    z, y, x = [lax.axis_index(name) for name in AXES]
    dist = jnp.abs(lane_of(8) - 64)
    line = jnp.zeros((8, 128), F32)
    for d in range(64):
        line = jnp.where(dist == d, top_taps[d], line)

    def inside(r, place, own, total):
        where = r + place * own
        return (where >= 0) & (where < total)

    def near(level, dist, keep):
        return jnp.where(keep, taps_at(taps, level, jnp.abs(dist)), 0.0)

    second = rows2[y]
    j, c = grid_of(128, 48)
    keep = (j < 64) & (c < 37) & inside(c - 2, y, 32, 128)
    right = jnp.where(keep, phi_at(y * 32 + c - 2 - 2 * j), 0.0).astype(BF16)
    for s in range(4):
        first = lax.rem(y + s, 4) * 16 - 2
        left = toeplitz(line, 24, -first)
        i, l = grid_of(24, 128)
        keep = (l < 64) & (i < 21) & (first + i >= 0) & (first + i < 64)
        full = exact_right(jnp.where(keep, left, 0.0), right)
        ytab[24 * s : 24 * s + 24, :] = exact_right(full, second)
    i, c = grid_of(72, 48)
    keep = (i < 37) & inside(i - 2, y, 32, 128)
    keep = keep | ((i >= 40) & (i < 53) & (y > 0)) | ((i >= 56) & (i < 69) & (y < 3))
    r = jnp.where(i < 40, i - 2, jnp.where(i < 56, i - 50, i - 26))
    ytab[96:168, :] = exact_right(near(2, r - (c - 2), keep), second)

    i, l = grid_of(128, 64)
    left = phi_at(x * 32 + i % 32 - 2 * l).astype(BF16)
    i, l = grid_of(64, 128)
    a, b = grid_of(128, 128)
    for s in range(4):
        first = lax.rem(x + s, 4) * 16 - 2
        right = toeplitz(line, 64, first)
        keep = (l < 21) & (first + l >= 0) & (first + l < 64)
        right = jnp.where(keep, right, 0.0)
        right = right + pltpu.roll(right, 32, 1)
        right = right + pltpu.roll(right, 64, 1)
        full = exact_left(left, right)
        ttab[:, 128 * s : 128 * s + 128] = jnp.where(a // 32 == b // 32, full, 0.0)
    i, l = grid_of(128, 256)
    r = l % 64 - 2
    keep = (l // 64 == i // 32) & (l % 64 < 37) & inside(r, x, 32, 128)
    ntab[:, 0:256] = near(2, r - i % 32, keep)
    i, l = grid_of(128, 128)
    same = l // 32 == i // 32
    ntab[:, 256:384] = near(2, l % 32 - 8 - i % 32, same & (l % 32 < 11) & (x > 0))
    ntab[:, 384:512] = near(2, l % 32 + 30 - i % 32, same & (l % 32 < 10) & (x < 3))

    i, l = grid_of(16, 64)
    left = phi_at(z * 16 + i - 2 * l).astype(BF16)
    i, l = grid_of(64, 128)
    parts = []
    for s in range(8):
        chip, core = lax.rem(z // 2 + s % 4, 4), lax.rem(z + s // 4, 2)
        first = (2 * chip + core) * 8 - 2
        right = toeplitz(line, 64, first)
        keep = (l < 13) & (first + l >= 0) & (first + l < 64)
        parts.append(exact_left(left, jnp.where(keep, right, 0.0)))
    whole = jnp.concatenate(parts, axis=0) * 0.125
    i, l = grid_of(128, 128)
    for quarter in range(4):
        spread = jnp.where(i == 4 * quarter + l // 32, 1.0, 0.0).astype(BF16)
        full = exact_right(whole, spread)
        for s in range(8):
            at = (s * 4 + quarter) * 16
            tcoef[at : at + 16, :] = full[16 * s : 16 * s + 16]
    i, l = grid_of(16, 128)
    g = l // 64
    for p in range(22):
        if p < 11:
            r = g + (2 * p - 2)
            keep = (r <= 18) & inside(r, z, 16, 128)
        elif p < 17:
            r = g + (2 * (p - 11) - 8)
            keep = (r <= 2) & (z > 0)
        else:
            r = g + (2 * (p - 17) + 14)
            keep = (r <= 23) & (z < 7)
        ncoef[16 * p : 16 * p + 16, :] = near(2, r - i, keep) * 0.25

    i, c = grid_of(104, 80)
    keep = (i < 67) & inside(i - 1, y, 64, 256)
    keep = keep | ((i >= 72) & (i < 83) & (y > 0)) | ((i >= 88) & (i < 99) & (y < 3))
    r = jnp.where(i < 72, i - 1, jnp.where(i < 88, i - 81, i - 25))
    oney[...] = exact_right(near(1, r - (c - 1), keep), rows1[y])
    i, l = grid_of(128, 256)
    r = l % 128 - 1
    keep = (l // 128 == i // 64) & (l % 128 < 67) & inside(r, x, 64, 256)
    onex[...] = near(1, r - i % 64, keep)
    i, l = grid_of(512, 128)
    same = l // 16 == i // 64
    edges[:, 0:128] = near(1, l % 16 - 8 - i % 64, same & (l % 16 < 10) & (x > 0))
    edges[:, 128:256] = near(1, l % 16 + 63 - i % 64, same & (l % 16 < 9) & (x < 3))


def tables(taps, top_taps, after):
    return call(
        tables_body,
        [
            (168, 128), (128, 512), (128, 512), (512, 128),
            (352, 128), (104, 128), (128, 256), (512, 256),
        ],
        us=2,
        in_specs=[SMEM, SMEM, VMEM, VMEM],
        out_specs=[VMEM] * 8,
        after=after,
    )(taps, top_taps, *[jnp.asarray(t) for t in chain_rows(512, 4)])


def rise_tables():
    def kron(table, groups):
        return np.stack([np.kron(np.eye(groups), t.T) for t in table])

    y2 = prolong_table(128, 4, 2, 3, 2, 3, (40, 24))
    x2 = kron(prolong_table(128, 4, 2, 3, 2, 3, (64, 32)), 4)
    y1 = prolong_table(256, 4, 1, 2, 2, 3, (72, 40))
    x1 = kron(prolong_table(256, 4, 1, 2, 2, 3, (128, 64)), 2)
    y0 = prolong_table(512, 4, 0, 0, 1, 2, (128, 72))
    x0 = kron(prolong_table(512, 4, 0, 0, 1, 2, (128, 128)), 1)
    mask2 = np.zeros((8, 11, 128), np.float32)
    mask1 = np.zeros((8, 35), np.float32)
    for place in range(8):
        for e in range(22):
            inside = 0 <= place * 16 - 2 + e < 128
            mask2[place, e // 2, 64 * (e % 2) : 64 * (e % 2) + 64] = inside
        for f in range(35):
            mask1[place, f] = 0 <= place * 32 - 1 + f < 256
    half = lambda table: jnp.asarray(table.astype(jnp.bfloat16))
    return half(y2), half(x2), jnp.asarray(mask2), half(y1), half(x1), jnp.asarray(mask1), half(y0), half(x0)


def per_device(charges, taps, top_taps):
    z, y, x = AXES
    chain = jnp.asarray(chain_tables(512, 4))

    one, two, low, high = coarse_z(charges)
    f_high, f_low = shift(low, z, -1), shift(high, z, 1)
    near, *nsides = near_z(taps, charges, (two,))
    nf_high, nf_low = shift(nsides[0], z, -1), shift(nsides[1], z, 1)
    ytab, ttab, ntab, tcoef, ncoef, oney, onex, edges = tables(taps, top_taps, (two,))

    one, two, low, high = coarse_x(chain, one, two, f_high, f_low, ())
    f_high, f_low = shift(low, x, -1), shift(high, x, 1)
    near, *nsides = near_x(taps, near, nf_high, nf_low, (two,))

    top, near2, near1, up, down, far, *nsides = top_y(ytab, oney, one, two, f_high, f_low, nsides)
    f_low, f_high, f_far = shift(up, y, 1), shift(down, y, -1), shift(far, y, 2)
    nf_high, nf_low = shift(nsides[0], x, -1), shift(nsides[1], x, 1)

    top, near2, near1, up, down, far = top_x(
        ttab, ntab, onex, edges, top, near2, near1, f_low, f_high, f_far, ()
    )
    f_low, f_high, f_far = shift(up, x, 1), shift(down, x, -1), shift(far, x, 2)
    near, *nsides = near_y(taps, near, nf_high, nf_low, (top,))

    top, partner, near2, near1, up, down = top_z(
        taps, tcoef, ncoef, top, near2, near1, f_low, f_high, f_far, (nsides[0],)
    )
    count = lax.axis_size(z)
    partner = lax.ppermute(partner, z, [(i, i ^ 1) for i in range(count)])
    f_low, f_high = shift(up, z, 1), shift(down, z, -1)
    nf_high, nf_low = shift(nsides[0], y, -1), shift(nsides[1], y, 1)
    top, *others = top_sum(top, partner, (nf_high, nf_low))
    others = [shift(part, z, 2 + 2 * k) for k, part in enumerate(others)]

    coarse = rise(rise_tables(), top, others, near2, f_low, f_high, near1)
    return finest(near, nf_high, nf_low, coarse)


def solution(mesh):
    return jax.shard_map(
        per_device,
        mesh=mesh,
        in_specs=(P("gz", "gy", "gx"), P(), P()),
        out_specs=P("gz", "gy", "gx"),
        check_vma=False,
    )
```

profile of v0, /device:TPU:1, one launch (start us, length us, event | category | flops | bytes accessed | tf_op | source)
XLA Modules:
  0.0 71.0 jit_solution(11535891613326410626)
XLA Ops:
  0.0 2.2 %copy-done = f32[64,128,128]{2,1,0:T(8,128)S(1)} copy-done((f32[64,128,128]{2,1,0:T(8,128)S(1)}, f32[64,128,128]{2,1,0:T(8,128)}, u32[]{:S(2)}) %copy-start) | copy-done | bytes 4194328
  2.2 0.8 %shard_map.136 = (f32[32,128,128]{2,1,0:T(8,128)S(1)}, f32[16,128,128]{2,1,0:T(8,128)S(1)}, f32[3,128,128]{2,1,0:T(8,128)S(1)}, f32[5,128,128]{2,1,0:T(8,128)S(1)}) custom-call(f32[64,128,128]{2,1,0:T(8,128)S(1)} %copy-done), custom_call_target="tpu_custom_call" | custom-call | flops 17250000896 | bytes 540000000 | tf_op jit(solution)/shard_map/pallas_call | solution.py:144
  3.0 2.6 %collective-permute-start.3 = (f32[5,128,128]{2,1,0:T(8,128)S(1)}, f32[5,128,128]{2,1,0:T(8,128)S(1)}, u32[]{:S(2)}, u32[]{:S(2)}) collective-permute-start(f32[5,128,128]{2,1,0:T(8,128)S(1)} %get-tuple-element.60), channel_id=1, source_target_pairs={{0,16},{16,32},{32,48},{48,64},{64,80},{80,96},{96,112},{112,0},{1... | collective-permute-start | bytes 983048 | tf_op jit(solution)/shard_map/ppermute | solution.py:88
  5.7 0.0 copy-start.11
  5.7 4.2 %shard_map.137 = (f32[64,128,128]{2,1,0:T(8,128)S(1)}, f32[8,128,128]{2,1,0:T(8,128)S(1)}, f32[8,128,128]{2,1,0:T(8,128)S(1)}) custom-call(f32[3,9]{1,0:T(4,128)S(1)} %copy-done.1, f32[64,128,128]{2,1,0:T(8,128)S(1)} %copy-done, f32[16,128,128]{2,1,0:T(8,128)S(1)} %get-tuple-element.54.refs_2_.refs_4_), custom_call_target="tpu_custom_call" | custom-call | flops 69000003584 | bytes 2160000000 | tf_op jit(solution)/shard_map/pallas_call | solution.py:144
  9.8 1.8 %collective-permute-start = (f32[8,128,128]{2,1,0:T(8,128)S(1)}, f32[8,128,128]{2,1,0:T(8,128)S(1)}, u32[]{:S(2)}, u32[]{:S(2)}) collective-permute-start(f32[8,128,128]{2,1,0:T(8,128)S(1)} %get-tuple-element.56), channel_id=1, source_target_pairs={{0,112},{16,0},{32,16},{48,32},{64,48},{80,64},{96,80},{112,96},{1... | collective-permute-start | bytes 1572872 | tf_op jit(solution)/shard_map/ppermute | solution.py:88
  11.6 0.0 collective-permute-start.1
  11.6 2.3 %shard_map.140 = (f32[168,128]{1,0:T(8,128)S(1)}, f32[128,512]{1,0:T(8,128)S(1)}, f32[128,512]{1,0:T(8,128)S(1)}, f32[512,128]{1,0:T(8,128)S(1)}, f32[352,128]{1...) custom-call(f32[3,9]{1,0:T(4,128)S(1)} %copy-done.1, f32[64]{0:T(128)S(1)} %copy-done.2, ...), custom_call_target="tpu_custom_call" | custom-call | flops 23000000512 | bytes 720000000 | tf_op jit(solution)/shard_map/pallas_call | solution.py:144
  14.0 0.0 collective-permute-done.2.refs_3_
  14.0 1.1 %shard_map.138 = (f32[32,64,128]{2,1,0:T(8,128)S(1)}, f32[16,32,128]{2,1,0:T(8,128)S(1)}, f32[24,8,128]{2,1,0:T(8,128)S(1)}, f32[24,8,128]{2,1,0:T(8,128)S(1)}) custom-call(bf16[4,128,128]{2,1,0:T(8,128)(2,1)S(1)} %copy-done.7, f32[32,128,128]{2,1,0:T(8,128)S(1)} %get-tuple-element.58.refs_1_, f32[16,128,128]{2,1,0:T(8,128)S(1)} %get-tuple-element.54.refs_2_.refs_4_, ...), custom_call_target="tpu_custom_call" | custom-call | flops 23000000512 | bytes 720000000 | tf_op jit(solution)/shard_map/pallas_call | solution.py:144
  15.1 3.9 %collective-permute-start.4 = (f32[24,8,128]{2,1,0:T(8,128)S(1)}, f32[24,8,128]{2,1,0:T(8,128)S(1)}, u32[]{:S(2)}, u32[]{:S(2)}) collective-permute-start(f32[24,8,128]{2,1,0:T(8,128)S(1)} %get-tuple-element.66), channel_id=1, source_target_pairs={{0,3},{1,0},{2,1},{3,2},{4,7},{5,4},{6,5},{7,6},{8,11},{9,8},{10,9... | collective-permute-start | bytes 294920 | tf_op jit(solution)/shard_map/ppermute | solution.py:88
  19.0 0.0 collective-permute-start.5
  19.0 0.0 collective-permute-done.refs_2_
  19.0 3.9 %shard_map.139 = (f32[64,128,128]{2,1,0:T(8,128)S(1)}, f32[4,128,128]{2,1,0:T(8,128)S(1)}, f32[4,128,128]{2,1,0:T(8,128)S(1)}) custom-call(f32[3,9]{1,0:T(4,128)S(1)} %copy-done.1, f32[64,128,128]{2,1,0:T(8,128)S(1)} %get-tuple-element.55.refs_1_, f32[8,128,128]{2,1,0:T(8,128)S(1)} %collective-permute-done.refs_2_, ...), custom_call_target="tpu_custom_call" | custom-call | flops 57500000256 | bytes 1800000000 | tf_op jit(solution)/shard_map/pallas_call | solution.py:144
  22.9 0.0 collective-permute-done.4.refs_4_
  22.9 0.7 %collective-permute-done.5.refs_5_ = f32[24,8,128]{2,1,0:T(8,128)S(1)} collective-permute-done((f32[24,8,128]{2,1,0:T(8,128)S(1)}, f32[24,8,128]{2,1,0:T(8,128)S(1)}, u32[]{:S(2)}, u32[]{:S(2)}) %collective-permute-start.5) | collective-permute-done | bytes 98336 | tf_op jit(solution)/shard_map/ppermute | solution.py:88
  23.7 0.8 %shard_map.141 = (f32[24,512]{1,0:T(8,128)S(1)}, f32[40,512]{1,0:T(8,128)S(1)}, f32[72,2048]{1,0:T(8,128)S(1)}, f32[104,512]{1,0:T(8,128)S(1)}, f32[104,512]{1,0...) custom-call(f32[168,128]{1,0:T(8,128)S(1)} %get-tuple-element.63.ref, ...), custom_call_target="tpu_custom_call", output_to_operand_aliasing={{6}: (6, {}), {7}: (7, {})} | custom-call | flops 17250000896 | bytes 540000000 | tf_op jit(solution)/shard_map/pallas_call | solution.py:144
  24.5 1.4 %collective-permute-start.8 = (f32[104,512]{1,0:T(8,128)S(1)}, f32[104,512]{1,0:T(8,128)S(1)}, u32[]{:S(2)}, u32[]{:S(2)}) collective-permute-start(f32[104,512]{1,0:T(8,128)S(1)} %get-tuple-element.79), channel_id=1, source_target_pairs={{0,4},{4,8},{8,12},{12,0},{1,5},{5,9},{9,13},{13,1},{2,6},{6,10},{... | collective-permute-start | bytes 638984 | tf_op jit(solution)/shard_map/ppermute | solution.py:88
  25.8 1.5 %collective-permute-start.9 = (f32[104,512]{1,0:T(8,128)S(1)}, f32[104,512]{1,0:T(8,128)S(1)}, u32[]{:S(2)}, u32[]{:S(2)}) collective-permute-start(f32[104,512]{1,0:T(8,128)S(1)} %get-tuple-element.80), channel_id=1, source_target_pairs={{0,12},{4,0},{8,4},{12,8},{1,13},{5,1},{9,5},{13,9},{2,14},{6,2},{... | collective-permute-start | bytes 638984 | tf_op jit(solution)/shard_map/ppermute | solution.py:88
  27.3 1.6 %collective-permute-start.10 = (f32[24,512]{1,0:T(8,128)S(1)}, f32[24,512]{1,0:T(8,128)S(1)}, u32[]{:S(2)}, u32[]{:S(2)}) collective-permute-start(f32[24,512]{1,0:T(8,128)S(1)} %get-tuple-element.81), channel_id=1, source_target_pairs={{0,8},{4,12},{8,0},{12,4},{1,9},{5,13},{9,1},{13,5},{2,10},{6,14},... | collective-permute-start | bytes 147464 | tf_op jit(solution)/shard_map/ppermute | solution.py:88
  28.9 2.8 %collective-permute-start.6 = (f32[4,128,128]{2,1,0:T(8,128)S(1)}, f32[4,128,128]{2,1,0:T(8,128)S(1)}, u32[]{:S(2)}, u32[]{:S(2)}) collective-permute-start(f32[4,128,128]{2,1,0:T(8,128)S(1)} %get-tuple-element.70), channel_id=1, source_target_pairs={{0,3},{1,0},{2,1},{3,2},{4,7},{5,4},{6,5},{7,6},{8,11},{9,8},{10,9... | collective-permute-start | bytes 786440 | tf_op jit(solution)/shard_map/ppermute | solution.py:88
  31.7 0.9 %collective-permute-done.10.refs_9_ = f32[24,512]{1,0:T(8,128)S(1)} collective-permute-done((f32[24,512]{1,0:T(8,128)S(1)}, f32[24,512]{1,0:T(8,128)S(1)}, u32[]{:S(2)}, u32[]{:S(2)}) %collective-permute-start.10) | collective-permute-done | bytes 49184 | tf_op jit(solution)/shard_map/ppermute | solution.py:88
  32.6 1.4 %shard_map.142 = (f32[96,128]{1,0:T(8,128)S(1)}, f32[160,256]{1,0:T(8,128)S(1)}, f32[32,72,128]{2,1,0:T(8,128)S(1)}, f32[544,128]{1,0:T(8,128)S(1)}, f32[544,128]{1,0:T(8,128)S(1)}, /*index=5*/f32[96,128]{1,0:T(8,128)S(1)}) custom-call(f32[128,512]{1,0:T(8,128)S(1)} %get-tuple-element.72.refs_0_, f32[128,512]{1,0:T(8,128)S(1)} %get-tuple-element.73.refs_1_, ...), custom_call_target="tpu_custom_call" | custom-call | flops 23000000512 | bytes 720000000 | tf_op jit(solution)/shard_map/pallas_call | solution.py:144
  34.0 0.5 collective-permute-start.13
  34.5 2.3 %collective-permute-start.14 = (f32[544,128]{1,0:T(8,128)S(1)}, f32[544,128]{1,0:T(8,128)S(1)}, u32[]{:S(2)}, u32[]{:S(2)}) collective-permute-start(f32[544,128]{1,0:T(8,128)S(1)} %get-tuple-element.91), channel_id=1, source_target_pairs={{0,3},{1,0},{2,1},{3,2},{4,7},{5,4},{6,5},{7,6},{8,11},{9,8},{10,9... | collective-permute-start | bytes 835592 | tf_op jit(solution)/shard_map/ppermute | solution.py:88
  36.8 1.1 %collective-permute-start.15 = (f32[96,128]{1,0:T(8,128)S(1)}, f32[96,128]{1,0:T(8,128)S(1)}, u32[]{:S(2)}, u32[]{:S(2)}) collective-permute-start(f32[96,128]{1,0:T(8,128)S(1)} %get-tuple-element.92), channel_id=1, source_target_pairs={{0,2},{1,3},{2,0},{3,1},{4,6},{5,7},{6,4},{7,5},{8,10},{9,11},{10,... | collective-permute-start | bytes 147464 | tf_op jit(solution)/shard_map/ppermute | solution.py:88
  37.9 0.2 collective-permute-done.7.refs_3_
  38.1 4.1 %shard_map.143 = (f32[64,128,128]{2,1,0:T(8,128)S(1)}, f32[64,8,128]{2,1,0:T(8,128)S(1)}, f32[64,8,128]{2,1,0:T(8,128)S(1)}) custom-call(f32[3,9]{1,0:T(4,128)S(1)} %copy-done.1, f32[64,128,128]{2,1,0:T(8,128)S(1)} %get-tuple-element.62.refs_1_, f32[4,128,128]{2,1,0:T(8,128)S(1)} %collective-permute-done.6.refs_2_, ...), custom_call_target="tpu_custom_call" | custom-call | flops 46000001024 | bytes 1440000000 | tf_op jit(solution)/shard_map/pallas_call | solution.py:144
  42.2 1.3 %collective-permute-start.11 = (f32[64,8,128]{2,1,0:T(8,128)S(1)}, f32[64,8,128]{2,1,0:T(8,128)S(1)}, u32[]{:S(2)}, u32[]{:S(2)}) collective-permute-start(f32[64,8,128]{2,1,0:T(8,128)S(1)} %get-tuple-element.84.refs_9_), channel_id=1, source_target_pairs={{0,12},{4,0},{8,4},{12,8},{1,13},{5,1},{9,5},{13,9},{2,14},{6,2},{... | collective-permute-start | bytes 786440 | tf_op jit(solution)/shard_map/ppermute | solution.py:88
  43.6 0.2 collective-permute-start.12
  43.8 1.9 %collective-permute-done.15.refs_8_ = f32[96,128]{1,0:T(8,128)S(1)} collective-permute-done((f32[96,128]{1,0:T(8,128)S(1)}, f32[96,128]{1,0:T(8,128)S(1)}, u32[]{:S(2)}, u32[]{:S(2)}) %collective-permute-start.15) | collective-permute-done | bytes 49184 | tf_op jit(solution)/shard_map/ppermute | solution.py:88
  45.6 4.4 %shard_map.144 = (f32[384,128]{1,0:T(8,128)S(1)}, f32[384,128]{1,0:T(8,128)S(1)}, f32[440,128]{1,0:T(8,128)S(1)}, f32[35,72,128]{2,1,0:T(8,128)S(1)}, f32[632,128]{1,0:T(8,128)S(1)}, /*index=5*/f32[672,128]{1,0:T(8,128)S(1)}) custom-call(f32[3,9]{1,0:T(4,128)S(1)} %copy-done.1, f32[512,128]{1,0:T(8,128)S(1)} %get-tuple-element.86.refs_1_, ...), custom_call_target="tpu_custom_call" | custom-call | flops 46000001024 | bytes 1440000000 | tf_op jit(solution)/shard_map/pallas_call | solution.py:144
  50.1 5.3 %collective-permute-start.16 = (f32[384,128]{1,0:T(8,128)S(1)}, f32[384,128]{1,0:T(8,128)S(1)}, u32[]{:S(2)}, u32[]{:S(2)}) collective-permute-start(f32[384,128]{1,0:T(8,128)S(1)} %get-tuple-element.94), channel_id=1, source_target_pairs={{0,16},{16,0},{32,48},{48,32},{64,80},{80,64},{96,112},{112,96},{1... | collective-permute-start | bytes 589832 | tf_op jit(solution)/shard_map/ppermute | solution.py:929
  55.3 0.0 collective-permute-start.21
  55.3 1.7 %collective-permute-start.20 = (f32[632,128]{1,0:T(8,128)S(1)}, f32[632,128]{1,0:T(8,128)S(1)}, u32[]{:S(2)}, u32[]{:S(2)}) collective-permute-start(f32[632,128]{1,0:T(8,128)S(1)} %get-tuple-element.100), channel_id=1, source_target_pairs={{0,16},{16,32},{32,48},{48,64},{64,80},{80,96},{96,112},{112,0},{1... | collective-permute-start | bytes 970760 | tf_op jit(solution)/shard_map/ppermute | solution.py:88
  57.1 0.0 copy-start.3
  57.1 0.0 copy-start.4
  57.1 0.0 copy-start.5
  57.1 0.0 copy-start.6
  57.1 0.0 copy-start.9
  57.1 0.0 copy-start.10
  57.2 0.0 copy-start.12
  57.2 0.0 copy-start.13
  57.2 0.1 collective-permute-start.17
  57.3 2.9 %collective-permute-start.18 = (f32[96,128]{1,0:T(8,128)S(1)}, f32[96,128]{1,0:T(8,128)S(1)}, u32[]{:S(2)}, u32[]{:S(2)}) collective-permute-start(f32[96,128]{1,0:T(8,128)S(1)} %get-tuple-element.97), channel_id=1, source_target_pairs={{0,64},{16,80},{32,96},{48,112},{64,0},{80,16},{96,32},{112,48},{1... | collective-permute-start | bytes 147464 | tf_op jit(solution)/shard_map/ppermute | solution.py:88
  60.2 5.1 %collective-permute-done.17.refs_9_ = f32[96,128]{1,0:T(8,128)S(1)} collective-permute-done((f32[96,128]{1,0:T(8,128)S(1)}, f32[96,128]{1,0:T(8,128)S(1)}, u32[]{:S(2)}, u32[]{:S(2)}) %collective-permute-start.17) | collective-permute-done | bytes 49184 | tf_op jit(solution)/shard_map/ppermute | solution.py:88
  65.4 3.0 %shard_map.146.refs_3_ = f32[35,128,128]{2,1,0:T(8,128)S(1)} custom-call(bf16[4,40,24]{2,1,0:T(8,128)(2,1)S(1)} %copy-done.12, bf16[4,128,256]{2,1,0:T(8,128)(2,1)S(1)} %copy-done.3, f32[8,11,128]{2,1,0:T(8,128)S(1)} %copy-done.10, bf16[4,72,40]{2,1,0:T(8,128)(2,1)S(1)} %copy-done.9, bf16[4,128,256]{2,1,0:T(8,128)(2,1)S(1)} %copy-done.4, ...), custom_call_target="tpu_custom_call" | custom-call | flops 57500000256 | bytes 1800000000 | tf_op jit(solution)/shard_map/pallas_call | solution.py:144
  68.4 2.6 %shard_map.147 = f32[64,128,128]{2,1,0:T(8,128)} custom-call(f32[64,128,128]{2,1,0:T(8,128)S(1)} %get-tuple-element.83.refs_0_, f32[64,8,128]{2,1,0:T(8,128)S(1)} %collective-permute-done.11.refs_2_.refs_1_, f32[64,8,128]{2,1,0:T(8,128)S(1)} %collective-permute-done.12.refs_3_.refs_2_, f32[35,128,128]{2,1,0:T(8,128)S(1)} %shard_map.146.refs_3_), custom_call_target="tpu_custom_call" | custom-call | flops 46000001024 | bytes 1440000000 | tf_op jit(solution)/shard_map/pallas_call | solution.py:144
  (36 shorter events, 0.1 us)
Async XLA Ops:
  0.0 2.2 %copy-start = (f32[64,128,128]{2,1,0:T(8,128)S(1)}, f32[64,128,128]{2,1,0:T(8,128)}, u32[]{:S(2)}) copy-start(f32[64,128,128]{2,1,0:T(8,128)} %refs_1_.3) | copy-start | bytes 12582916
  2.2 3.5 %copy-start.1 = (f32[3,9]{1,0:T(4,128)S(1)}, f32[3,9]{1,0:T(4,128)}, u32[]{:S(2)}) copy-start(f32[3,9]{1,0:T(4,128)} %refs_0_.13) | copy-start | bytes 328
  3.0 10.9 %collective-permute-start.3 = (f32[5,128,128]{2,1,0:T(8,128)S(1)}, f32[5,128,128]{2,1,0:T(8,128)S(1)}, u32[]{:S(2)}, u32[]{:S(2)}) collective-permute-start(f32[5,128,128]{2,1,0:T(8,128)S(1)} %get-tuple-element.60), channel_id=1, source_target_pairs={{0,16},{16,32},{32,48},{48,64},{64,80},{80,96},{96,112},{112,0},{1... | collective-permute-start | bytes 983048 | tf_op jit(solution)/shard_map/ppermute | solution.py:88
  5.6 8.3 %collective-permute-start.2 = (f32[3,128,128]{2,1,0:T(8,128)S(1)}, f32[3,128,128]{2,1,0:T(8,128)S(1)}, u32[]{:S(2)}, u32[]{:S(2)}) collective-permute-start(f32[3,128,128]{2,1,0:T(8,128)S(1)} %get-tuple-element.59), channel_id=1, source_target_pairs={{0,112},{16,0},{32,16},{48,32},{64,48},{80,64},{96,80},{112,96},{1... | collective-permute-start | bytes 589832 | tf_op jit(solution)/shard_map/ppermute | solution.py:88
  5.7 6.0 %copy-start.2 = (f32[64]{0:T(128)S(1)}, f32[64]{0:T(128)}, u32[]{:S(2)}) copy-start(f32[64]{0:T(128)} %refs_1_.4) | copy-start | bytes 772
  5.7 6.0 %copy-start.8 = (bf16[4,80,128]{2,1,0:T(8,128)(2,1)S(1)}, bf16[4,80,128]{2,1,0:T(8,128)(2,1)}, u32[]{:S(2)}) copy-start(bf16[4,80,128]{2,1,0:T(8,128)(2,1)} %constant.23.clone.refs_2_) | copy-start | bytes 245764
  5.7 6.0 %copy-start.11 = (bf16[4,48,128]{2,1,0:T(8,128)(2,1)S(1)}, bf16[4,48,128]{2,1,0:T(8,128)(2,1)}, u32[]{:S(2)}) copy-start(bf16[4,48,128]{2,1,0:T(8,128)(2,1)} %constant.24.clone.refs_3_) | copy-start | bytes 147460
  9.8 9.2 %collective-permute-start = (f32[8,128,128]{2,1,0:T(8,128)S(1)}, f32[8,128,128]{2,1,0:T(8,128)S(1)}, u32[]{:S(2)}, u32[]{:S(2)}) collective-permute-start(f32[8,128,128]{2,1,0:T(8,128)S(1)} %get-tuple-element.56), channel_id=1, source_target_pairs={{0,112},{16,0},{32,16},{48,32},{64,48},{80,64},{96,80},{112,96},{1... | collective-permute-start | bytes 1572872 | tf_op jit(solution)/shard_map/ppermute | solution.py:88
  11.6 2.4 %copy-start.7 = (bf16[4,128,128]{2,1,0:T(8,128)(2,1)S(1)}, bf16[4,128,128]{2,1,0:T(8,128)(2,1)}, u32[]{:S(2)}) copy-start(bf16[4,128,128]{2,1,0:T(8,128)(2,1)} %constant.22.clone.refs_0_) | copy-start | bytes 393220
  11.6 7.4 %collective-permute-start.1 = (f32[8,128,128]{2,1,0:T(8,128)S(1)}, f32[8,128,128]{2,1,0:T(8,128)S(1)}, u32[]{:S(2)}, u32[]{:S(2)}) collective-permute-start(f32[8,128,128]{2,1,0:T(8,128)S(1)} %get-tuple-element.57), channel_id=1, source_target_pairs={{0,16},{16,32},{32,48},{48,64},{64,80},{80,96},{96,112},{112,0},{1... | collective-permute-start | bytes 1572872 | tf_op jit(solution)/shard_map/ppermute | solution.py:88
  15.1 7.8 %collective-permute-start.4 = (f32[24,8,128]{2,1,0:T(8,128)S(1)}, f32[24,8,128]{2,1,0:T(8,128)S(1)}, u32[]{:S(2)}, u32[]{:S(2)}) collective-permute-start(f32[24,8,128]{2,1,0:T(8,128)S(1)} %get-tuple-element.66), channel_id=1, source_target_pairs={{0,3},{1,0},{2,1},{3,2},{4,7},{5,4},{6,5},{7,6},{8,11},{9,8},{10,9... | collective-permute-start | bytes 294920 | tf_op jit(solution)/shard_map/ppermute | solution.py:88
  19.0 4.7 %collective-permute-start.5 = (f32[24,8,128]{2,1,0:T(8,128)S(1)}, f32[24,8,128]{2,1,0:T(8,128)S(1)}, u32[]{:S(2)}, u32[]{:S(2)}) collective-permute-start(f32[24,8,128]{2,1,0:T(8,128)S(1)} %get-tuple-element.67), channel_id=1, source_target_pairs={{0,1},{1,2},{2,3},{3,0},{4,5},{5,6},{6,7},{7,4},{8,9},{9,10},{10,1... | collective-permute-start | bytes 294920 | tf_op jit(solution)/shard_map/ppermute | solution.py:88
  24.5 8.1 %collective-permute-start.8 = (f32[104,512]{1,0:T(8,128)S(1)}, f32[104,512]{1,0:T(8,128)S(1)}, u32[]{:S(2)}, u32[]{:S(2)}) collective-permute-start(f32[104,512]{1,0:T(8,128)S(1)} %get-tuple-element.79), channel_id=1, source_target_pairs={{0,4},{4,8},{8,12},{12,0},{1,5},{5,9},{9,13},{13,1},{2,6},{6,10},{... | collective-permute-start | bytes 638984 | tf_op jit(solution)/shard_map/ppermute | solution.py:88
  25.8 6.7 %collective-permute-start.9 = (f32[104,512]{1,0:T(8,128)S(1)}, f32[104,512]{1,0:T(8,128)S(1)}, u32[]{:S(2)}, u32[]{:S(2)}) collective-permute-start(f32[104,512]{1,0:T(8,128)S(1)} %get-tuple-element.80), channel_id=1, source_target_pairs={{0,12},{4,0},{8,4},{12,8},{1,13},{5,1},{9,5},{13,9},{2,14},{6,2},{... | collective-permute-start | bytes 638984 | tf_op jit(solution)/shard_map/ppermute | solution.py:88
  27.3 5.2 %collective-permute-start.10 = (f32[24,512]{1,0:T(8,128)S(1)}, f32[24,512]{1,0:T(8,128)S(1)}, u32[]{:S(2)}, u32[]{:S(2)}) collective-permute-start(f32[24,512]{1,0:T(8,128)S(1)} %get-tuple-element.81), channel_id=1, source_target_pairs={{0,8},{4,12},{8,0},{12,4},{1,9},{5,13},{9,1},{13,5},{2,10},{6,14},... | collective-permute-start | bytes 147464 | tf_op jit(solution)/shard_map/ppermute | solution.py:88
  28.9 9.0 %collective-permute-start.6 = (f32[4,128,128]{2,1,0:T(8,128)S(1)}, f32[4,128,128]{2,1,0:T(8,128)S(1)}, u32[]{:S(2)}, u32[]{:S(2)}) collective-permute-start(f32[4,128,128]{2,1,0:T(8,128)S(1)} %get-tuple-element.70), channel_id=1, source_target_pairs={{0,3},{1,0},{2,1},{3,2},{4,7},{5,4},{6,5},{7,6},{8,11},{9,8},{10,9... | collective-permute-start | bytes 786440 | tf_op jit(solution)/shard_map/ppermute | solution.py:88
  31.7 6.4 %collective-permute-start.7 = (f32[4,128,128]{2,1,0:T(8,128)S(1)}, f32[4,128,128]{2,1,0:T(8,128)S(1)}, u32[]{:S(2)}, u32[]{:S(2)}) collective-permute-start(f32[4,128,128]{2,1,0:T(8,128)S(1)} %get-tuple-element.71), channel_id=1, source_target_pairs={{0,1},{1,2},{2,3},{3,0},{4,5},{5,6},{6,7},{7,4},{8,9},{9,10},{10,1... | collective-permute-start | bytes 786440 | tf_op jit(solution)/shard_map/ppermute | solution.py:88
  34.0 11.6 %collective-permute-start.13 = (f32[544,128]{1,0:T(8,128)S(1)}, f32[544,128]{1,0:T(8,128)S(1)}, u32[]{:S(2)}, u32[]{:S(2)}) collective-permute-start(f32[544,128]{1,0:T(8,128)S(1)} %get-tuple-element.90), channel_id=1, source_target_pairs={{0,1},{1,2},{2,3},{3,0},{4,5},{5,6},{6,7},{7,4},{8,9},{9,10},{10,1... | collective-permute-start | bytes 835592 | tf_op jit(solution)/shard_map/ppermute | solution.py:88
  34.5 11.2 %collective-permute-start.14 = (f32[544,128]{1,0:T(8,128)S(1)}, f32[544,128]{1,0:T(8,128)S(1)}, u32[]{:S(2)}, u32[]{:S(2)}) collective-permute-start(f32[544,128]{1,0:T(8,128)S(1)} %get-tuple-element.91), channel_id=1, source_target_pairs={{0,3},{1,0},{2,1},{3,2},{4,7},{5,4},{6,5},{7,6},{8,11},{9,8},{10,9... | collective-permute-start | bytes 835592 | tf_op jit(solution)/shard_map/ppermute | solution.py:88
  36.8 8.9 %collective-permute-start.15 = (f32[96,128]{1,0:T(8,128)S(1)}, f32[96,128]{1,0:T(8,128)S(1)}, u32[]{:S(2)}, u32[]{:S(2)}) collective-permute-start(f32[96,128]{1,0:T(8,128)S(1)} %get-tuple-element.92), channel_id=1, source_target_pairs={{0,2},{1,3},{2,0},{3,1},{4,6},{5,7},{6,4},{7,5},{8,10},{9,11},{10,... | collective-permute-start | bytes 147464 | tf_op jit(solution)/shard_map/ppermute | solution.py:88
  42.2 14.8 %collective-permute-start.11 = (f32[64,8,128]{2,1,0:T(8,128)S(1)}, f32[64,8,128]{2,1,0:T(8,128)S(1)}, u32[]{:S(2)}, u32[]{:S(2)}) collective-permute-start(f32[64,8,128]{2,1,0:T(8,128)S(1)} %get-tuple-element.84.refs_9_), channel_id=1, source_target_pairs={{0,12},{4,0},{8,4},{12,8},{1,13},{5,1},{9,5},{13,9},{2,14},{6,2},{... | collective-permute-start | bytes 786440 | tf_op jit(solution)/shard_map/ppermute | solution.py:88
  43.6 13.5 %collective-permute-start.12 = (f32[64,8,128]{2,1,0:T(8,128)S(1)}, f32[64,8,128]{2,1,0:T(8,128)S(1)}, u32[]{:S(2)}, u32[]{:S(2)}) collective-permute-start(f32[64,8,128]{2,1,0:T(8,128)S(1)} %get-tuple-element.85), channel_id=1, source_target_pairs={{0,4},{4,8},{8,12},{12,0},{1,5},{5,9},{9,13},{13,1},{2,6},{6,10},{... | collective-permute-start | bytes 786440 | tf_op jit(solution)/shard_map/ppermute | solution.py:88
  50.1 7.0 %collective-permute-start.16 = (f32[384,128]{1,0:T(8,128)S(1)}, f32[384,128]{1,0:T(8,128)S(1)}, u32[]{:S(2)}, u32[]{:S(2)}) collective-permute-start(f32[384,128]{1,0:T(8,128)S(1)} %get-tuple-element.94), channel_id=1, source_target_pairs={{0,16},{16,0},{32,48},{48,32},{64,80},{80,64},{96,112},{112,96},{1... | collective-permute-start | bytes 589832 | tf_op jit(solution)/shard_map/ppermute | solution.py:929
  55.3 10.0 %collective-permute-start.21 = (f32[672,128]{1,0:T(8,128)S(1)}, f32[672,128]{1,0:T(8,128)S(1)}, u32[]{:S(2)}, u32[]{:S(2)}) collective-permute-start(f32[672,128]{1,0:T(8,128)S(1)} %get-tuple-element.101), channel_id=1, source_target_pairs={{0,112},{16,0},{32,16},{48,32},{64,48},{80,64},{96,80},{112,96},{1... | collective-permute-start | bytes 1032200 | tf_op jit(solution)/shard_map/ppermute | solution.py:88
  55.3 9.9 %collective-permute-start.20 = (f32[632,128]{1,0:T(8,128)S(1)}, f32[632,128]{1,0:T(8,128)S(1)}, u32[]{:S(2)}, u32[]{:S(2)}) collective-permute-start(f32[632,128]{1,0:T(8,128)S(1)} %get-tuple-element.100), channel_id=1, source_target_pairs={{0,16},{16,32},{32,48},{48,64},{64,80},{80,96},{96,112},{112,0},{1... | collective-permute-start | bytes 970760 | tf_op jit(solution)/shard_map/ppermute | solution.py:88
  57.1 8.2 %copy-start.3 = (bf16[4,128,256]{2,1,0:T(8,128)(2,1)S(1)}, bf16[4,128,256]{2,1,0:T(8,128)(2,1)}, u32[]{:S(2)}) copy-start(bf16[4,128,256]{2,1,0:T(8,128)(2,1)} %constant.26.clone.refs_1_) | copy-start | bytes 786436
  57.1 8.2 %copy-start.4 = (bf16[4,128,256]{2,1,0:T(8,128)(2,1)S(1)}, bf16[4,128,256]{2,1,0:T(8,128)(2,1)}, u32[]{:S(2)}) copy-start(bf16[4,128,256]{2,1,0:T(8,128)(2,1)} %constant.29.clone.refs_4_) | copy-start | bytes 786436
  57.1 8.2 %copy-start.5 = (bf16[4,128,72]{2,1,0:T(8,128)(2,1)S(1)}, bf16[4,128,72]{2,1,0:T(8,128)(2,1)}, u32[]{:S(2)}) copy-start(bf16[4,128,72]{2,1,0:T(8,128)(2,1)} %constant.31.clone.refs_6_) | copy-start | bytes 221188
  57.1 8.2 %copy-start.6 = (bf16[4,128,128]{2,1,0:T(8,128)(2,1)S(1)}, bf16[4,128,128]{2,1,0:T(8,128)(2,1)}, u32[]{:S(2)}) copy-start(bf16[4,128,128]{2,1,0:T(8,128)(2,1)} %constant.32.clone.refs_7_) | copy-start | bytes 393220
  57.1 8.2 %copy-start.9 = (bf16[4,72,40]{2,1,0:T(8,128)(2,1)S(1)}, bf16[4,72,40]{2,1,0:T(8,128)(2,1)}, u32[]{:S(2)}) copy-start(bf16[4,72,40]{2,1,0:T(8,128)(2,1)} %constant.28.clone.refs_3_) | copy-start | bytes 69124
  57.1 8.2 %copy-start.10 = (f32[8,11,128]{2,1,0:T(8,128)S(1)}, f32[8,11,128]{2,1,0:T(8,128)}, u32[]{:S(2)}) copy-start(f32[8,11,128]{2,1,0:T(8,128)} %constant.27.clone.refs_2_) | copy-start | bytes 135172
  57.2 8.2 %copy-start.12 = (bf16[4,40,24]{2,1,0:T(8,128)(2,1)S(1)}, bf16[4,40,24]{2,1,0:T(8,128)(2,1)}, u32[]{:S(2)}) copy-start(bf16[4,40,24]{2,1,0:T(8,128)(2,1)} %constant.25.clone.refs_0_) | copy-start | bytes 23044
  57.2 8.2 %copy-start.13 = (f32[8,35]{1,0:T(8,128)S(1)}, f32[8,35]{1,0:T(8,128)}, u32[]{:S(2)}) copy-start(f32[8,35]{1,0:T(8,128)} %constant.30.clone.refs_5_) | copy-start | bytes 3364
  57.2 8.1 %collective-permute-start.17 = (f32[96,128]{1,0:T(8,128)S(1)}, f32[96,128]{1,0:T(8,128)S(1)}, u32[]{:S(2)}, u32[]{:S(2)}) collective-permute-start(f32[96,128]{1,0:T(8,128)S(1)} %get-tuple-element.96), channel_id=1, source_target_pairs={{0,32},{16,48},{32,64},{48,80},{64,96},{80,112},{96,0},{112,16},{1... | collective-permute-start | bytes 147464 | tf_op jit(solution)/shard_map/ppermute | solution.py:88
  57.3 8.0 %collective-permute-start.18 = (f32[96,128]{1,0:T(8,128)S(1)}, f32[96,128]{1,0:T(8,128)S(1)}, u32[]{:S(2)}, u32[]{:S(2)}) collective-permute-start(f32[96,128]{1,0:T(8,128)S(1)} %get-tuple-element.97), channel_id=1, source_target_pairs={{0,64},{16,80},{32,96},{48,112},{64,0},{80,16},{96,32},{112,48},{1... | collective-permute-start | bytes 147464 | tf_op jit(solution)/shard_map/ppermute | solution.py:88
  60.2 5.1 %collective-permute-start.19 = (f32[96,128]{1,0:T(8,128)S(1)}, f32[96,128]{1,0:T(8,128)S(1)}, u32[]{:S(2)}, u32[]{:S(2)}) collective-permute-start(f32[96,128]{1,0:T(8,128)S(1)} %get-tuple-element.98), channel_id=1, source_target_pairs={{0,96},{16,112},{32,0},{48,16},{64,32},{80,48},{96,64},{112,80},{1... | collective-permute-start | bytes 147464 | tf_op jit(solution)/shard_map/ppermute | solution.py:88
where the time goes:
time: 71.1 us; the launch traced here: 71 us
  starting transfers between devices  30.9 us (43%)
  Pallas kernels  28.7 us (40%)
  waiting for transfers between devices  8.87 us (12%)
  local copies, waits for them, and re-layouts  2.26 us (3%)
    pallas_call x12, Pallas kernels, call(): return lambda *args: kernel(*args, *after, *carry)  28.7 us
    ppermute x21, starting transfers between devices, shift(): lax.ppermute(value, name, [(i, (i + step) % count) for i in range(count)])  25.6 us
    ppermute x21, waiting for transfers between devices, shift(): lax.ppermute(value, name, [(i, (i + step) % count) for i in range(count)])  8.87 us
    ppermute x1, starting transfers between devices, per_device(): partner = lax.ppermute(partner, z, [(i, i ^ 1) for i in range(count)])  5.26 us
    unnamed x28, local copies, waits for them, and re-layouts  2.26 us
  transfers between devices with their start and end apart: 22, of which 5 were waited for; matrix products, arithmetic and copies ran while one was open for 0% of the time, Pallas kernels for 30%

commit v1 on v0

--- a/solution.py
+++ b/solution.py
@@ -647,7 +647,8 @@
         first, second = split(value)
         full = dot(jnp.concatenate([first, second], axis=1), table) + dot(first, lower)
         own[k] = full[:, 0:128]
-        low[q, :, 8 * j : 8 * j + 8] = full[:, 128:136]
+        at = 8 * ((j - 1) % 16)
+        low[q, :, at : at + 8] = full[:, 128:136]
         high[q, :, 8 * j : 8 * j + 8] = full[:, 136:144]
 
     for j in range(16):
@@ -690,10 +691,9 @@
     lane = lane_of(128)
 
     def load(q, j):
-        left = pltpu.roll(from_low[q], (128 - 8 * j) % 128, 1)
-        right = pltpu.roll(from_high[q], (120 - 8 * j) % 128, 1)
-        sides = jnp.where(lane < 8, left, jnp.where(lane >= 120, right, 0.0))
-        return g[16 * q + j] + sides
+        sides = jnp.where(lane // 8 == j, from_low[q], from_high[q])
+        sides = pltpu.roll(sides, (128 - 8 * j) % 128, 1) if j else sides
+        return g[16 * q + j] + jnp.where((lane < 8) | (lane >= 120), sides, 0.0)
 
     @pl.loop(0, 4)
     def _(q):
@@ -724,17 +724,17 @@
 
 def finest_body(near, from_high, from_low, coarse, out):
     step = pl.program_id(0)
-    at = 8 * step
-    planes = [coarse[at + h] for h in range(11)]
-    for k in range(16):
+    at = 16 * step
+    planes = [coarse[at + h] for h in range(19)]
+    for k in range(32):
         h = k // 2
         value = planes[h + 1]
         if k % 2:
             value = 0.5625 * (value + planes[h + 2]) - 0.0625 * (planes[h] + planes[h + 3])
-        value = value + near[16 * step + k]
-        out[k, 0:8] = value[0:8] + from_low[16 * step + k]
+        value = value + near[32 * step + k]
+        out[k, 0:8] = value[0:8] + from_low[32 * step + k]
         out[k, 8:120] = value[8:120]
-        out[k, 120:128] = value[120:128] + from_high[16 * step + k]
+        out[k, 120:128] = value[120:128] + from_high[32 * step + k]
 
 
 def finest(near, from_high, from_low, coarse):
@@ -743,9 +743,9 @@
         [(64, 128, 128)],
         us=4,
         vmem=16,
-        grid=(4,),
+        grid=(2,),
         in_specs=[VMEM] * 4,
-        out_specs=[pl.BlockSpec((16, 128, 128), lambda i: (i, 0, 0))],
+        out_specs=[pl.BlockSpec((32, 128, 128), lambda i: (i, 0, 0))],
     )(near, from_high, from_low, coarse)[0]
 
 

time: 71.1 us -> 70.7 us (level)
  Pallas kernels: 28.7 us -> 27.2 us
  waiting for transfers between devices: 8.87 us -> 10.2 us
    pallas_call x12, Pallas kernels: 28.7 us -> 27.2 us  [call(): return lambda *args: kernel(*args, *after, *carry)]
    ppermute x21, waiting for transfers between devices: 8.87 us -> 10.2 us  [shift(): lax.ppermute(value, name, [(i, (i + step) % count) for i in range(count)])]
    ppermute x1, starting transfers between devices: 5.26 us -> 4.16 us  [per_device(): partner = lax.ppermute(partner, z, [(i, i ^ 1) for i in range(count)])]
    ppermute x21, starting transfers between devices: 25.6 us -> 26.5 us  [shift(): lax.ppermute(value, name, [(i, (i + step) % count) for i in range(count)])]
  transfers between devices with their start and end apart: 22 -> 22, of which waited for: 5 -> 5; matrix products, arithmetic and copies ran while one was open for 0% -> 0% of each run, Pallas kernels for 30% -> 29%
where the time goes in v1:
time: 70.7 us; the launch traced here: 70.6 us
  starting transfers between devices  30.6 us (43%)
  Pallas kernels  27.2 us (38%)
  waiting for transfers between devices  10.2 us (14%)
  local copies, waits for them, and re-layouts  2.26 us (3%)
    pallas_call x12, Pallas kernels, call(): return lambda *args: kernel(*args, *after, *carry)  27.2 us
    ppermute x21, starting transfers between devices, shift(): lax.ppermute(value, name, [(i, (i + step) % count) for i in range(count)])  26.5 us
    ppermute x21, waiting for transfers between devices, shift(): lax.ppermute(value, name, [(i, (i + step) % count) for i in range(count)])  10.2 us
    ppermute x1, starting transfers between devices, per_device(): partner = lax.ppermute(partner, z, [(i, i ^ 1) for i in range(count)])  4.16 us
    unnamed x28, local copies, waits for them, and re-layouts  2.26 us
  transfers between devices with their start and end apart: 22, of which 5 were waited for; matrix products, arithmetic and copies ran while one was open for 0% of the time, Pallas kernels for 29%

profile of v1, /device:TPU:1, one launch (start us, length us, event | category | flops | bytes accessed | tf_op | source)
XLA Modules:
  0.0 70.6 jit_solution(10027482813202326054)
XLA Ops:
  0.0 2.2 %copy-done = f32[64,128,128]{2,1,0:T(8,128)S(1)} copy-done((f32[64,128,128]{2,1,0:T(8,128)S(1)}, f32[64,128,128]{2,1,0:T(8,128)}, u32[]{:S(2)}) %copy-start) | copy-done | bytes 4194328
  2.2 0.8 %shard_map.136 = (f32[32,128,128]{2,1,0:T(8,128)S(1)}, f32[16,128,128]{2,1,0:T(8,128)S(1)}, f32[3,128,128]{2,1,0:T(8,128)S(1)}, f32[5,128,128]{2,1,0:T(8,128)S(1)}) custom-call(f32[64,128,128]{2,1,0:T(8,128)S(1)} %copy-done), custom_call_target="tpu_custom_call" | custom-call | flops 17250000896 | bytes 540000000 | tf_op jit(solution)/shard_map/pallas_call | solution.py:144
  3.0 2.6 %collective-permute-start.3 = (f32[5,128,128]{2,1,0:T(8,128)S(1)}, f32[5,128,128]{2,1,0:T(8,128)S(1)}, u32[]{:S(2)}, u32[]{:S(2)}) collective-permute-start(f32[5,128,128]{2,1,0:T(8,128)S(1)} %get-tuple-element.60), channel_id=1, source_target_pairs={{0,16},{16,32},{32,48},{48,64},{64,80},{80,96},{96,112},{112,0},{1... | collective-permute-start | bytes 983048 | tf_op jit(solution)/shard_map/ppermute | solution.py:88
  5.7 0.0 copy-start.11
  5.7 4.2 %shard_map.137 = (f32[64,128,128]{2,1,0:T(8,128)S(1)}, f32[8,128,128]{2,1,0:T(8,128)S(1)}, f32[8,128,128]{2,1,0:T(8,128)S(1)}) custom-call(f32[3,9]{1,0:T(4,128)S(1)} %copy-done.1, f32[64,128,128]{2,1,0:T(8,128)S(1)} %copy-done, f32[16,128,128]{2,1,0:T(8,128)S(1)} %get-tuple-element.54.refs_2_.refs_4_), custom_call_target="tpu_custom_call" | custom-call | flops 69000003584 | bytes 2160000000 | tf_op jit(solution)/shard_map/pallas_call | solution.py:144
  9.8 1.8 %collective-permute-start = (f32[8,128,128]{2,1,0:T(8,128)S(1)}, f32[8,128,128]{2,1,0:T(8,128)S(1)}, u32[]{:S(2)}, u32[]{:S(2)}) collective-permute-start(f32[8,128,128]{2,1,0:T(8,128)S(1)} %get-tuple-element.56), channel_id=1, source_target_pairs={{0,112},{16,0},{32,16},{48,32},{64,48},{80,64},{96,80},{112,96},{1... | collective-permute-start | bytes 1572872 | tf_op jit(solution)/shard_map/ppermute | solution.py:88
  11.6 0.0 collective-permute-start.1
  11.6 2.3 %shard_map.140 = (f32[168,128]{1,0:T(8,128)S(1)}, f32[128,512]{1,0:T(8,128)S(1)}, f32[128,512]{1,0:T(8,128)S(1)}, f32[512,128]{1,0:T(8,128)S(1)}, f32[352,128]{1...) custom-call(f32[3,9]{1,0:T(4,128)S(1)} %copy-done.1, f32[64]{0:T(128)S(1)} %copy-done.2, ...), custom_call_target="tpu_custom_call" | custom-call | flops 23000000512 | bytes 720000000 | tf_op jit(solution)/shard_map/pallas_call | solution.py:144
  14.0 0.0 collective-permute-done.3.refs_4_
  14.0 1.1 %shard_map.138 = (f32[32,64,128]{2,1,0:T(8,128)S(1)}, f32[16,32,128]{2,1,0:T(8,128)S(1)}, f32[24,8,128]{2,1,0:T(8,128)S(1)}, f32[24,8,128]{2,1,0:T(8,128)S(1)}) custom-call(bf16[4,128,128]{2,1,0:T(8,128)(2,1)S(1)} %copy-done.7, f32[32,128,128]{2,1,0:T(8,128)S(1)} %get-tuple-element.58.refs_1_, f32[16,128,128]{2,1,0:T(8,128)S(1)} %get-tuple-element.54.refs_2_.refs_4_, ...), custom_call_target="tpu_custom_call" | custom-call | flops 23000000512 | bytes 720000000 | tf_op jit(solution)/shard_map/pallas_call | solution.py:144
  15.1 3.9 %collective-permute-start.4 = (f32[24,8,128]{2,1,0:T(8,128)S(1)}, f32[24,8,128]{2,1,0:T(8,128)S(1)}, u32[]{:S(2)}, u32[]{:S(2)}) collective-permute-start(f32[24,8,128]{2,1,0:T(8,128)S(1)} %get-tuple-element.66), channel_id=1, source_target_pairs={{0,3},{1,0},{2,1},{3,2},{4,7},{5,4},{6,5},{7,6},{8,11},{9,8},{10,9... | collective-permute-start | bytes 294920 | tf_op jit(solution)/shard_map/ppermute | solution.py:88
  19.0 0.0 collective-permute-start.5
  19.0 0.0 collective-permute-done.refs_2_
  19.0 0.0 collective-permute-done.1.refs_3_
  19.0 3.8 %shard_map.139 = (f32[64,128,128]{2,1,0:T(8,128)S(1)}, f32[4,128,128]{2,1,0:T(8,128)S(1)}, f32[4,128,128]{2,1,0:T(8,128)S(1)}) custom-call(f32[3,9]{1,0:T(4,128)S(1)} %copy-done.1, f32[64,128,128]{2,1,0:T(8,128)S(1)} %get-tuple-element.55.refs_1_, f32[8,128,128]{2,1,0:T(8,128)S(1)} %collective-permute-done.refs_2_, ...), custom_call_target="tpu_custom_call" | custom-call | flops 57500000256 | bytes 1800000000 | tf_op jit(solution)/shard_map/pallas_call | solution.py:144
  22.8 0.9 %collective-permute-done.5.refs_5_ = f32[24,8,128]{2,1,0:T(8,128)S(1)} collective-permute-done((f32[24,8,128]{2,1,0:T(8,128)S(1)}, f32[24,8,128]{2,1,0:T(8,128)S(1)}, u32[]{:S(2)}, u32[]{:S(2)}) %collective-permute-start.5) | collective-permute-done | bytes 98336 | tf_op jit(solution)/shard_map/ppermute | solution.py:88
  23.7 0.8 %shard_map.141 = (f32[24,512]{1,0:T(8,128)S(1)}, f32[40,512]{1,0:T(8,128)S(1)}, f32[72,2048]{1,0:T(8,128)S(1)}, f32[104,512]{1,0:T(8,128)S(1)}, f32[104,512]{1,0...) custom-call(f32[168,128]{1,0:T(8,128)S(1)} %get-tuple-element.63.ref, ...), custom_call_target="tpu_custom_call", output_to_operand_aliasing={{6}: (6, {}), {7}: (7, {})} | custom-call | flops 17250000896 | bytes 540000000 | tf_op jit(solution)/shard_map/pallas_call | solution.py:144
  24.5 1.4 %collective-permute-start.8 = (f32[104,512]{1,0:T(8,128)S(1)}, f32[104,512]{1,0:T(8,128)S(1)}, u32[]{:S(2)}, u32[]{:S(2)}) collective-permute-start(f32[104,512]{1,0:T(8,128)S(1)} %get-tuple-element.79), channel_id=1, source_target_pairs={{0,4},{4,8},{8,12},{12,0},{1,5},{5,9},{9,13},{13,1},{2,6},{6,10},{... | collective-permute-start | bytes 638984 | tf_op jit(solution)/shard_map/ppermute | solution.py:88
  25.8 1.5 %collective-permute-start.9 = (f32[104,512]{1,0:T(8,128)S(1)}, f32[104,512]{1,0:T(8,128)S(1)}, u32[]{:S(2)}, u32[]{:S(2)}) collective-permute-start(f32[104,512]{1,0:T(8,128)S(1)} %get-tuple-element.80), channel_id=1, source_target_pairs={{0,12},{4,0},{8,4},{12,8},{1,13},{5,1},{9,5},{13,9},{2,14},{6,2},{... | collective-permute-start | bytes 638984 | tf_op jit(solution)/shard_map/ppermute | solution.py:88
  27.3 1.6 %collective-permute-start.10 = (f32[24,512]{1,0:T(8,128)S(1)}, f32[24,512]{1,0:T(8,128)S(1)}, u32[]{:S(2)}, u32[]{:S(2)}) collective-permute-start(f32[24,512]{1,0:T(8,128)S(1)} %get-tuple-element.81), channel_id=1, source_target_pairs={{0,8},{4,12},{8,0},{12,4},{1,9},{5,13},{9,1},{13,5},{2,10},{6,14},... | collective-permute-start | bytes 147464 | tf_op jit(solution)/shard_map/ppermute | solution.py:88
  28.9 2.6 %collective-permute-start.6 = (f32[4,128,128]{2,1,0:T(8,128)S(1)}, f32[4,128,128]{2,1,0:T(8,128)S(1)}, u32[]{:S(2)}, u32[]{:S(2)}) collective-permute-start(f32[4,128,128]{2,1,0:T(8,128)S(1)} %get-tuple-element.70), channel_id=1, source_target_pairs={{0,3},{1,0},{2,1},{3,2},{4,7},{5,4},{6,5},{7,6},{8,11},{9,8},{10,9... | collective-permute-start | bytes 786440 | tf_op jit(solution)/shard_map/ppermute | solution.py:88
  31.5 1.0 %collective-permute-done.10.refs_9_ = f32[24,512]{1,0:T(8,128)S(1)} collective-permute-done((f32[24,512]{1,0:T(8,128)S(1)}, f32[24,512]{1,0:T(8,128)S(1)}, u32[]{:S(2)}, u32[]{:S(2)}) %collective-permute-start.10) | collective-permute-done | bytes 49184 | tf_op jit(solution)/shard_map/ppermute | solution.py:88
  32.6 1.4 %shard_map.142 = (f32[96,128]{1,0:T(8,128)S(1)}, f32[160,256]{1,0:T(8,128)S(1)}, f32[32,72,128]{2,1,0:T(8,128)S(1)}, f32[544,128]{1,0:T(8,128)S(1)}, f32[544,128]{1,0:T(8,128)S(1)}, /*index=5*/f32[96,128]{1,0:T(8,128)S(1)}) custom-call(f32[128,512]{1,0:T(8,128)S(1)} %get-tuple-element.72.refs_0_, f32[128,512]{1,0:T(8,128)S(1)} %get-tuple-element.73.refs_1_, ...), custom_call_target="tpu_custom_call" | custom-call | flops 23000000512 | bytes 720000000 | tf_op jit(solution)/shard_map/pallas_call | solution.py:144
  34.0 0.3 collective-permute-start.13
  34.3 2.4 %collective-permute-start.14 = (f32[544,128]{1,0:T(8,128)S(1)}, f32[544,128]{1,0:T(8,128)S(1)}, u32[]{:S(2)}, u32[]{:S(2)}) collective-permute-start(f32[544,128]{1,0:T(8,128)S(1)} %get-tuple-element.91), channel_id=1, source_target_pairs={{0,3},{1,0},{2,1},{3,2},{4,7},{5,4},{6,5},{7,6},{8,11},{9,8},{10,9... | collective-permute-start | bytes 835592 | tf_op jit(solution)/shard_map/ppermute | solution.py:88
  36.8 1.0 %collective-permute-start.15 = (f32[96,128]{1,0:T(8,128)S(1)}, f32[96,128]{1,0:T(8,128)S(1)}, u32[]{:S(2)}, u32[]{:S(2)}) collective-permute-start(f32[96,128]{1,0:T(8,128)S(1)} %get-tuple-element.92), channel_id=1, source_target_pairs={{0,2},{1,3},{2,0},{3,1},{4,6},{5,7},{6,4},{7,5},{8,10},{9,11},{10,... | collective-permute-start | bytes 147464 | tf_op jit(solution)/shard_map/ppermute | solution.py:88
  37.8 0.2 collective-permute-done.7.refs_3_
  38.0 3.0 %shard_map.143 = (f32[64,128,128]{2,1,0:T(8,128)S(1)}, f32[64,8,128]{2,1,0:T(8,128)S(1)}, f32[64,8,128]{2,1,0:T(8,128)S(1)}) custom-call(f32[3,9]{1,0:T(4,128)S(1)} %copy-done.1, f32[64,128,128]{2,1,0:T(8,128)S(1)} %get-tuple-element.62.refs_1_, f32[4,128,128]{2,1,0:T(8,128)S(1)} %collective-permute-done.6.refs_2_, ...), custom_call_target="tpu_custom_call" | custom-call | flops 46000001024 | bytes 1440000000 | tf_op jit(solution)/shard_map/pallas_call | solution.py:144
  41.0 1.3 %collective-permute-start.11 = (f32[64,8,128]{2,1,0:T(8,128)S(1)}, f32[64,8,128]{2,1,0:T(8,128)S(1)}, u32[]{:S(2)}, u32[]{:S(2)}) collective-permute-start(f32[64,8,128]{2,1,0:T(8,128)S(1)} %get-tuple-element.84.refs_9_), channel_id=1, source_target_pairs={{0,12},{4,0},{8,4},{12,8},{1,13},{5,1},{9,5},{13,9},{2,14},{6,2},{... | collective-permute-start | bytes 786440 | tf_op jit(solution)/shard_map/ppermute | solution.py:88
  42.3 0.2 collective-permute-start.12
  42.5 3.0 %collective-permute-done.15.refs_8_ = f32[96,128]{1,0:T(8,128)S(1)} collective-permute-done((f32[96,128]{1,0:T(8,128)S(1)}, f32[96,128]{1,0:T(8,128)S(1)}, u32[]{:S(2)}, u32[]{:S(2)}) %collective-permute-start.15) | collective-permute-done | bytes 49184 | tf_op jit(solution)/shard_map/ppermute | solution.py:88
  45.5 4.4 %shard_map.144 = (f32[384,128]{1,0:T(8,128)S(1)}, f32[384,128]{1,0:T(8,128)S(1)}, f32[440,128]{1,0:T(8,128)S(1)}, f32[35,72,128]{2,1,0:T(8,128)S(1)}, f32[632,128]{1,0:T(8,128)S(1)}, /*index=5*/f32[672,128]{1,0:T(8,128)S(1)}) custom-call(f32[3,9]{1,0:T(4,128)S(1)} %copy-done.1, f32[512,128]{1,0:T(8,128)S(1)} %get-tuple-element.86.refs_1_, ...), custom_call_target="tpu_custom_call" | custom-call | flops 46000001024 | bytes 1440000000 | tf_op jit(solution)/shard_map/pallas_call | solution.py:144
  49.9 4.2 %collective-permute-start.16 = (f32[384,128]{1,0:T(8,128)S(1)}, f32[384,128]{1,0:T(8,128)S(1)}, u32[]{:S(2)}, u32[]{:S(2)}) collective-permute-start(f32[384,128]{1,0:T(8,128)S(1)} %get-tuple-element.94), channel_id=1, source_target_pairs={{0,16},{16,0},{32,48},{48,32},{64,80},{80,64},{96,112},{112,96},{1... | collective-permute-start | bytes 589832 | tf_op jit(solution)/shard_map/ppermute | solution.py:929
  54.1 0.0 collective-permute-start.21
  54.1 1.7 %collective-permute-start.20 = (f32[632,128]{1,0:T(8,128)S(1)}, f32[632,128]{1,0:T(8,128)S(1)}, u32[]{:S(2)}, u32[]{:S(2)}) collective-permute-start(f32[632,128]{1,0:T(8,128)S(1)} %get-tuple-element.100), channel_id=1, source_target_pairs={{0,16},{16,32},{32,48},{48,64},{64,80},{80,96},{96,112},{112,0},{1... | collective-permute-start | bytes 970760 | tf_op jit(solution)/shard_map/ppermute | solution.py:88
  55.9 0.0 copy-start.3
  55.9 0.0 copy-start.4
  55.9 0.0 copy-start.5
  55.9 0.0 copy-start.6
  55.9 0.0 copy-start.9
  55.9 0.0 copy-start.10
  55.9 0.0 copy-start.12
  55.9 0.0 copy-start.13
  56.0 0.2 collective-permute-start.17
  56.2 3.9 %collective-permute-start.18 = (f32[96,128]{1,0:T(8,128)S(1)}, f32[96,128]{1,0:T(8,128)S(1)}, u32[]{:S(2)}, u32[]{:S(2)}) collective-permute-start(f32[96,128]{1,0:T(8,128)S(1)} %get-tuple-element.97), channel_id=1, source_target_pairs={{0,64},{16,80},{32,96},{48,112},{64,0},{80,16},{96,32},{112,48},{1... | collective-permute-start | bytes 147464 | tf_op jit(solution)/shard_map/ppermute | solution.py:88
  60.0 5.1 %collective-permute-done.17.refs_9_ = f32[96,128]{1,0:T(8,128)S(1)} collective-permute-done((f32[96,128]{1,0:T(8,128)S(1)}, f32[96,128]{1,0:T(8,128)S(1)}, u32[]{:S(2)}, u32[]{:S(2)}) %collective-permute-start.17) | collective-permute-done | bytes 49184 | tf_op jit(solution)/shard_map/ppermute | solution.py:88
  65.3 3.0 %shard_map.146.refs_3_ = f32[35,128,128]{2,1,0:T(8,128)S(1)} custom-call(bf16[4,40,24]{2,1,0:T(8,128)(2,1)S(1)} %copy-done.12, bf16[4,128,256]{2,1,0:T(8,128)(2,1)S(1)} %copy-done.3, f32[8,11,128]{2,1,0:T(8,128)S(1)} %copy-done.10, bf16[4,72,40]{2,1,0:T(8,128)(2,1)S(1)} %copy-done.9, bf16[4,128,256]{2,1,0:T(8,128)(2,1)S(1)} %copy-done.4, ...), custom_call_target="tpu_custom_call" | custom-call | flops 57500000256 | bytes 1800000000 | tf_op jit(solution)/shard_map/pallas_call | solution.py:144
  68.2 2.4 %shard_map.147 = f32[64,128,128]{2,1,0:T(8,128)} custom-call(f32[64,128,128]{2,1,0:T(8,128)S(1)} %get-tuple-element.83.refs_0_, f32[64,8,128]{2,1,0:T(8,128)S(1)} %collective-permute-done.11.refs_2_.refs_1_, f32[64,8,128]{2,1,0:T(8,128)S(1)} %collective-permute-done.12.refs_3_.refs_2_, f32[35,128,128]{2,1,0:T(8,128)S(1)} %shard_map.146.refs_3_), custom_call_target="tpu_custom_call" | custom-call | flops 46000001024 | bytes 1440000000 | tf_op jit(solution)/shard_map/pallas_call | solution.py:144
  (36 shorter events, 0.1 us)
Async XLA Ops:
  0.0 2.2 %copy-start = (f32[64,128,128]{2,1,0:T(8,128)S(1)}, f32[64,128,128]{2,1,0:T(8,128)}, u32[]{:S(2)}) copy-start(f32[64,128,128]{2,1,0:T(8,128)} %refs_1_.3) | copy-start | bytes 12582916
  2.2 3.5 %copy-start.1 = (f32[3,9]{1,0:T(4,128)S(1)}, f32[3,9]{1,0:T(4,128)}, u32[]{:S(2)}) copy-start(f32[3,9]{1,0:T(4,128)} %refs_0_.13) | copy-start | bytes 328
  3.0 10.9 %collective-permute-start.3 = (f32[5,128,128]{2,1,0:T(8,128)S(1)}, f32[5,128,128]{2,1,0:T(8,128)S(1)}, u32[]{:S(2)}, u32[]{:S(2)}) collective-permute-start(f32[5,128,128]{2,1,0:T(8,128)S(1)} %get-tuple-element.60), channel_id=1, source_target_pairs={{0,16},{16,32},{32,48},{48,64},{64,80},{80,96},{96,112},{112,0},{1... | collective-permute-start | bytes 983048 | tf_op jit(solution)/shard_map/ppermute | solution.py:88
  5.6 8.3 %collective-permute-start.2 = (f32[3,128,128]{2,1,0:T(8,128)S(1)}, f32[3,128,128]{2,1,0:T(8,128)S(1)}, u32[]{:S(2)}, u32[]{:S(2)}) collective-permute-start(f32[3,128,128]{2,1,0:T(8,128)S(1)} %get-tuple-element.59), channel_id=1, source_target_pairs={{0,112},{16,0},{32,16},{48,32},{64,48},{80,64},{96,80},{112,96},{1... | collective-permute-start | bytes 589832 | tf_op jit(solution)/shard_map/ppermute | solution.py:88
  5.7 6.0 %copy-start.2 = (f32[64]{0:T(128)S(1)}, f32[64]{0:T(128)}, u32[]{:S(2)}) copy-start(f32[64]{0:T(128)} %refs_1_.4) | copy-start | bytes 772
  5.7 6.0 %copy-start.8 = (bf16[4,80,128]{2,1,0:T(8,128)(2,1)S(1)}, bf16[4,80,128]{2,1,0:T(8,128)(2,1)}, u32[]{:S(2)}) copy-start(bf16[4,80,128]{2,1,0:T(8,128)(2,1)} %constant.23.clone.refs_2_) | copy-start | bytes 245764
  5.7 6.0 %copy-start.11 = (bf16[4,48,128]{2,1,0:T(8,128)(2,1)S(1)}, bf16[4,48,128]{2,1,0:T(8,128)(2,1)}, u32[]{:S(2)}) copy-start(bf16[4,48,128]{2,1,0:T(8,128)(2,1)} %constant.24.clone.refs_3_) | copy-start | bytes 147460
  9.8 9.2 %collective-permute-start = (f32[8,128,128]{2,1,0:T(8,128)S(1)}, f32[8,128,128]{2,1,0:T(8,128)S(1)}, u32[]{:S(2)}, u32[]{:S(2)}) collective-permute-start(f32[8,128,128]{2,1,0:T(8,128)S(1)} %get-tuple-element.56), channel_id=1, source_target_pairs={{0,112},{16,0},{32,16},{48,32},{64,48},{80,64},{96,80},{112,96},{1... | collective-permute-start | bytes 1572872 | tf_op jit(solution)/shard_map/ppermute | solution.py:88
  11.6 2.4 %copy-start.7 = (bf16[4,128,128]{2,1,0:T(8,128)(2,1)S(1)}, bf16[4,128,128]{2,1,0:T(8,128)(2,1)}, u32[]{:S(2)}) copy-start(bf16[4,128,128]{2,1,0:T(8,128)(2,1)} %constant.22.clone.refs_0_) | copy-start | bytes 393220
  11.6 7.4 %collective-permute-start.1 = (f32[8,128,128]{2,1,0:T(8,128)S(1)}, f32[8,128,128]{2,1,0:T(8,128)S(1)}, u32[]{:S(2)}, u32[]{:S(2)}) collective-permute-start(f32[8,128,128]{2,1,0:T(8,128)S(1)} %get-tuple-element.57), channel_id=1, source_target_pairs={{0,16},{16,32},{32,48},{48,64},{64,80},{80,96},{96,112},{112,0},{1... | collective-permute-start | bytes 1572872 | tf_op jit(solution)/shard_map/ppermute | solution.py:88
  15.1 7.7 %collective-permute-start.4 = (f32[24,8,128]{2,1,0:T(8,128)S(1)}, f32[24,8,128]{2,1,0:T(8,128)S(1)}, u32[]{:S(2)}, u32[]{:S(2)}) collective-permute-start(f32[24,8,128]{2,1,0:T(8,128)S(1)} %get-tuple-element.66), channel_id=1, source_target_pairs={{0,3},{1,0},{2,1},{3,2},{4,7},{5,4},{6,5},{7,6},{8,11},{9,8},{10,9... | collective-permute-start | bytes 294920 | tf_op jit(solution)/shard_map/ppermute | solution.py:88
  19.0 4.7 %collective-permute-start.5 = (f32[24,8,128]{2,1,0:T(8,128)S(1)}, f32[24,8,128]{2,1,0:T(8,128)S(1)}, u32[]{:S(2)}, u32[]{:S(2)}) collective-permute-start(f32[24,8,128]{2,1,0:T(8,128)S(1)} %get-tuple-element.67), channel_id=1, source_target_pairs={{0,1},{1,2},{2,3},{3,0},{4,5},{5,6},{6,7},{7,4},{8,9},{9,10},{10,1... | collective-permute-start | bytes 294920 | tf_op jit(solution)/shard_map/ppermute | solution.py:88
  24.5 8.1 %collective-permute-start.8 = (f32[104,512]{1,0:T(8,128)S(1)}, f32[104,512]{1,0:T(8,128)S(1)}, u32[]{:S(2)}, u32[]{:S(2)}) collective-permute-start(f32[104,512]{1,0:T(8,128)S(1)} %get-tuple-element.79), channel_id=1, source_target_pairs={{0,4},{4,8},{8,12},{12,0},{1,5},{5,9},{9,13},{13,1},{2,6},{6,10},{... | collective-permute-start | bytes 638984 | tf_op jit(solution)/shard_map/ppermute | solution.py:88
  25.8 6.7 %collective-permute-start.9 = (f32[104,512]{1,0:T(8,128)S(1)}, f32[104,512]{1,0:T(8,128)S(1)}, u32[]{:S(2)}, u32[]{:S(2)}) collective-permute-start(f32[104,512]{1,0:T(8,128)S(1)} %get-tuple-element.80), channel_id=1, source_target_pairs={{0,12},{4,0},{8,4},{12,8},{1,13},{5,1},{9,5},{13,9},{2,14},{6,2},{... | collective-permute-start | bytes 638984 | tf_op jit(solution)/shard_map/ppermute | solution.py:88
  27.3 5.2 %collective-permute-start.10 = (f32[24,512]{1,0:T(8,128)S(1)}, f32[24,512]{1,0:T(8,128)S(1)}, u32[]{:S(2)}, u32[]{:S(2)}) collective-permute-start(f32[24,512]{1,0:T(8,128)S(1)} %get-tuple-element.81), channel_id=1, source_target_pairs={{0,8},{4,12},{8,0},{12,4},{1,9},{5,13},{9,1},{13,5},{2,10},{6,14},... | collective-permute-start | bytes 147464 | tf_op jit(solution)/shard_map/ppermute | solution.py:88
  28.9 8.9 %collective-permute-start.6 = (f32[4,128,128]{2,1,0:T(8,128)S(1)}, f32[4,128,128]{2,1,0:T(8,128)S(1)}, u32[]{:S(2)}, u32[]{:S(2)}) collective-permute-start(f32[4,128,128]{2,1,0:T(8,128)S(1)} %get-tuple-element.70), channel_id=1, source_target_pairs={{0,3},{1,0},{2,1},{3,2},{4,7},{5,4},{6,5},{7,6},{8,11},{9,8},{10,9... | collective-permute-start | bytes 786440 | tf_op jit(solution)/shard_map/ppermute | solution.py:88
  31.5 6.4 %collective-permute-start.7 = (f32[4,128,128]{2,1,0:T(8,128)S(1)}, f32[4,128,128]{2,1,0:T(8,128)S(1)}, u32[]{:S(2)}, u32[]{:S(2)}) collective-permute-start(f32[4,128,128]{2,1,0:T(8,128)S(1)} %get-tuple-element.71), channel_id=1, source_target_pairs={{0,1},{1,2},{2,3},{3,0},{4,5},{5,6},{6,7},{7,4},{8,9},{9,10},{10,1... | collective-permute-start | bytes 786440 | tf_op jit(solution)/shard_map/ppermute | solution.py:88
  34.0 11.5 %collective-permute-start.13 = (f32[544,128]{1,0:T(8,128)S(1)}, f32[544,128]{1,0:T(8,128)S(1)}, u32[]{:S(2)}, u32[]{:S(2)}) collective-permute-start(f32[544,128]{1,0:T(8,128)S(1)} %get-tuple-element.90), channel_id=1, source_target_pairs={{0,1},{1,2},{2,3},{3,0},{4,5},{5,6},{6,7},{7,4},{8,9},{9,10},{10,1... | collective-permute-start | bytes 835592 | tf_op jit(solution)/shard_map/ppermute | solution.py:88
  34.3 11.2 %collective-permute-start.14 = (f32[544,128]{1,0:T(8,128)S(1)}, f32[544,128]{1,0:T(8,128)S(1)}, u32[]{:S(2)}, u32[]{:S(2)}) collective-permute-start(f32[544,128]{1,0:T(8,128)S(1)} %get-tuple-element.91), channel_id=1, source_target_pairs={{0,3},{1,0},{2,1},{3,2},{4,7},{5,4},{6,5},{7,6},{8,11},{9,8},{10,9... | collective-permute-start | bytes 835592 | tf_op jit(solution)/shard_map/ppermute | solution.py:88
  36.8 8.8 %collective-permute-start.15 = (f32[96,128]{1,0:T(8,128)S(1)}, f32[96,128]{1,0:T(8,128)S(1)}, u32[]{:S(2)}, u32[]{:S(2)}) collective-permute-start(f32[96,128]{1,0:T(8,128)S(1)} %get-tuple-element.92), channel_id=1, source_target_pairs={{0,2},{1,3},{2,0},{3,1},{4,6},{5,7},{6,4},{7,5},{8,10},{9,11},{10,... | collective-permute-start | bytes 147464 | tf_op jit(solution)/shard_map/ppermute | solution.py:88
  41.0 14.8 %collective-permute-start.11 = (f32[64,8,128]{2,1,0:T(8,128)S(1)}, f32[64,8,128]{2,1,0:T(8,128)S(1)}, u32[]{:S(2)}, u32[]{:S(2)}) collective-permute-start(f32[64,8,128]{2,1,0:T(8,128)S(1)} %get-tuple-element.84.refs_9_), channel_id=1, source_target_pairs={{0,12},{4,0},{8,4},{12,8},{1,13},{5,1},{9,5},{13,9},{2,14},{6,2},{... | collective-permute-start | bytes 786440 | tf_op jit(solution)/shard_map/ppermute | solution.py:88
  42.3 13.5 %collective-permute-start.12 = (f32[64,8,128]{2,1,0:T(8,128)S(1)}, f32[64,8,128]{2,1,0:T(8,128)S(1)}, u32[]{:S(2)}, u32[]{:S(2)}) collective-permute-start(f32[64,8,128]{2,1,0:T(8,128)S(1)} %get-tuple-element.85), channel_id=1, source_target_pairs={{0,4},{4,8},{8,12},{12,0},{1,5},{5,9},{9,13},{13,1},{2,6},{6,10},{... | collective-permute-start | bytes 786440 | tf_op jit(solution)/shard_map/ppermute | solution.py:88
  49.9 5.9 %collective-permute-start.16 = (f32[384,128]{1,0:T(8,128)S(1)}, f32[384,128]{1,0:T(8,128)S(1)}, u32[]{:S(2)}, u32[]{:S(2)}) collective-permute-start(f32[384,128]{1,0:T(8,128)S(1)} %get-tuple-element.94), channel_id=1, source_target_pairs={{0,16},{16,0},{32,48},{48,32},{64,80},{80,64},{96,112},{112,96},{1... | collective-permute-start | bytes 589832 | tf_op jit(solution)/shard_map/ppermute | solution.py:929
  54.1 11.1 %collective-permute-start.21 = (f32[672,128]{1,0:T(8,128)S(1)}, f32[672,128]{1,0:T(8,128)S(1)}, u32[]{:S(2)}, u32[]{:S(2)}) collective-permute-start(f32[672,128]{1,0:T(8,128)S(1)} %get-tuple-element.101), channel_id=1, source_target_pairs={{0,112},{16,0},{32,16},{48,32},{64,48},{80,64},{96,80},{112,96},{1... | collective-permute-start | bytes 1032200 | tf_op jit(solution)/shard_map/ppermute | solution.py:88
  54.1 11.0 %collective-permute-start.20 = (f32[632,128]{1,0:T(8,128)S(1)}, f32[632,128]{1,0:T(8,128)S(1)}, u32[]{:S(2)}, u32[]{:S(2)}) collective-permute-start(f32[632,128]{1,0:T(8,128)S(1)} %get-tuple-element.100), channel_id=1, source_target_pairs={{0,16},{16,32},{32,48},{48,64},{64,80},{80,96},{96,112},{112,0},{1... | collective-permute-start | bytes 970760 | tf_op jit(solution)/shard_map/ppermute | solution.py:88
  55.9 9.3 %copy-start.3 = (bf16[4,128,256]{2,1,0:T(8,128)(2,1)S(1)}, bf16[4,128,256]{2,1,0:T(8,128)(2,1)}, u32[]{:S(2)}) copy-start(bf16[4,128,256]{2,1,0:T(8,128)(2,1)} %constant.26.clone.refs_1_) | copy-start | bytes 786436
  55.9 9.3 %copy-start.4 = (bf16[4,128,256]{2,1,0:T(8,128)(2,1)S(1)}, bf16[4,128,256]{2,1,0:T(8,128)(2,1)}, u32[]{:S(2)}) copy-start(bf16[4,128,256]{2,1,0:T(8,128)(2,1)} %constant.29.clone.refs_4_) | copy-start | bytes 786436
  55.9 9.3 %copy-start.5 = (bf16[4,128,72]{2,1,0:T(8,128)(2,1)S(1)}, bf16[4,128,72]{2,1,0:T(8,128)(2,1)}, u32[]{:S(2)}) copy-start(bf16[4,128,72]{2,1,0:T(8,128)(2,1)} %constant.31.clone.refs_6_) | copy-start | bytes 221188
  55.9 9.3 %copy-start.6 = (bf16[4,128,128]{2,1,0:T(8,128)(2,1)S(1)}, bf16[4,128,128]{2,1,0:T(8,128)(2,1)}, u32[]{:S(2)}) copy-start(bf16[4,128,128]{2,1,0:T(8,128)(2,1)} %constant.32.clone.refs_7_) | copy-start | bytes 393220
  55.9 9.3 %copy-start.9 = (bf16[4,72,40]{2,1,0:T(8,128)(2,1)S(1)}, bf16[4,72,40]{2,1,0:T(8,128)(2,1)}, u32[]{:S(2)}) copy-start(bf16[4,72,40]{2,1,0:T(8,128)(2,1)} %constant.28.clone.refs_3_) | copy-start | bytes 69124
  55.9 9.3 %copy-start.10 = (f32[8,11,128]{2,1,0:T(8,128)S(1)}, f32[8,11,128]{2,1,0:T(8,128)}, u32[]{:S(2)}) copy-start(f32[8,11,128]{2,1,0:T(8,128)} %constant.27.clone.refs_2_) | copy-start | bytes 135172
  55.9 9.3 %copy-start.12 = (bf16[4,40,24]{2,1,0:T(8,128)(2,1)S(1)}, bf16[4,40,24]{2,1,0:T(8,128)(2,1)}, u32[]{:S(2)}) copy-start(bf16[4,40,24]{2,1,0:T(8,128)(2,1)} %constant.25.clone.refs_0_) | copy-start | bytes 23044
  55.9 9.3 %copy-start.13 = (f32[8,35]{1,0:T(8,128)S(1)}, f32[8,35]{1,0:T(8,128)}, u32[]{:S(2)}) copy-start(f32[8,35]{1,0:T(8,128)} %constant.30.clone.refs_5_) | copy-start | bytes 3364
  56.0 9.2 %collective-permute-start.17 = (f32[96,128]{1,0:T(8,128)S(1)}, f32[96,128]{1,0:T(8,128)S(1)}, u32[]{:S(2)}, u32[]{:S(2)}) collective-permute-start(f32[96,128]{1,0:T(8,128)S(1)} %get-tuple-element.96), channel_id=1, source_target_pairs={{0,32},{16,48},{32,64},{48,80},{64,96},{80,112},{96,0},{112,16},{1... | collective-permute-start | bytes 147464 | tf_op jit(solution)/shard_map/ppermute | solution.py:88
  56.2 9.0 %collective-permute-start.18 = (f32[96,128]{1,0:T(8,128)S(1)}, f32[96,128]{1,0:T(8,128)S(1)}, u32[]{:S(2)}, u32[]{:S(2)}) collective-permute-start(f32[96,128]{1,0:T(8,128)S(1)} %get-tuple-element.97), channel_id=1, source_target_pairs={{0,64},{16,80},{32,96},{48,112},{64,0},{80,16},{96,32},{112,48},{1... | collective-permute-start | bytes 147464 | tf_op jit(solution)/shard_map/ppermute | solution.py:88
  60.0 5.1 %collective-permute-start.19 = (f32[96,128]{1,0:T(8,128)S(1)}, f32[96,128]{1,0:T(8,128)S(1)}, u32[]{:S(2)}, u32[]{:S(2)}) collective-permute-start(f32[96,128]{1,0:T(8,128)S(1)} %get-tuple-element.98), channel_id=1, source_target_pairs={{0,96},{16,112},{32,0},{48,16},{64,32},{80,48},{96,64},{112,80},{1... | collective-permute-start | bytes 147464 | tf_op jit(solution)/shard_map/ppermute | solution.py:88
